TPU v7x, 32 devices: a whole 2x2x4 slice. The times are simulated.
32 devices in a mesh: rep: 4 (over y, x), ep: 8 (over z, core).
Axes of the slice: x: 2, y: 2, z: 4, core: 2. Of those that a mesh axis runs over, the one named last changes fastest.
Arguments:
- tokens: bfloat16 [1024, 2048], P('ep', 'rep'), may hold values from -6 to 6
- out_grad: bfloat16 [1024, 2048], P('ep', 'rep'), may hold values from -6 to 6
- expert_ids: int32 [1024, 8], P('ep'), may hold values from 0 to 127, all different within a row; in each aligned block of 128 rows (0 to 127, 128 to 255, ...) at most 9 rows name the same one
- route_weight: bfloat16 [1024, 8], P('ep'), may hold values from 0.019897461 to 0.29882812
- w_gate: bfloat16 [128, 2048, 640], P('ep', 'rep'), may hold values from -0.125 to 0.125
- w_up: bfloat16 [128, 2048, 640], P('ep', 'rep'), may hold values from -0.125 to 0.125
- w_down: bfloat16 [128, 640, 2048], P('ep', None, 'rep'), may hold values from -0.25 to 0.25
Outputs:
- token_grad: bfloat16 [1024, 2048], P('ep', 'rep')
- grad_gate: bfloat16 [128, 2048, 640], P('ep', 'rep')
- grad_up: bfloat16 [128, 2048, 640], P('ep', 'rep')
- grad_down: bfloat16 [128, 640, 2048], P('ep', None, 'rep')
Inputs may be any that keep to these rules, and one draw needn't show every extreme that they name: `expert_ids`: each token picks 8 different experts. Among the 128 tokens of one index of ep no expert is picked by more than 9 tokens, and in every draw some expert is picked by exactly 9 tokens of some such index.
All inputs are finite; a program needn't handle non-finite values.
Results may differ from a plain program's by a relative error of at most 0.024.
Values may be sent and summed in bfloat16 or wider, within the bound.
A program may use at most 128 MiB of HBM per device.

v0:
```python
import jax
import jax.numpy as jnp
from jax import lax
from jax.sharding import PartitionSpec as P

CAP = 9


def hidden_terms(pre_gate, pre_up, pre_back, weight):
    sigmoid_gate = jax.nn.sigmoid(pre_gate)
    silu_gate = pre_gate * sigmoid_gate
    d_hidden = weight[..., None] * pre_back
    hidden = (silu_gate * pre_up).astype(jnp.bfloat16)
    gate_delta = (
        d_hidden * pre_up * sigmoid_gate * (1.0 + pre_gate * (1.0 - sigmoid_gate))
    ).astype(jnp.bfloat16)
    up_delta = (d_hidden * silu_gate).astype(jnp.bfloat16)
    return (hidden, gate_delta, up_delta)


def body(tokens, out_grad, expert_ids, route_weight, w_gate, w_up, w_down):
    ep_ranks = lax.axis_size("ep")
    local_count = w_gate.shape[0]
    experts = local_count * ep_ranks
    quarter = tokens.shape[1]
    slot_rows = ep_ranks * CAP
    slot_total = experts * CAP
    expert_range = jnp.arange(experts, dtype=jnp.int32)
    matches = expert_ids[:, :, None] == expert_range[None, None, :]
    picked = jnp.sum(matches.astype(jnp.int32), axis=1)
    before = jnp.cumsum(picked, axis=0) - picked
    position = jnp.sum(jnp.where(matches, before[:, None, :], 0), axis=2)
    owner_col = expert_ids // local_count
    within = expert_ids % local_count
    slot_index = (within * ep_ranks + owner_col) * CAP + position
    select = slot_index[:, :, None] == jnp.arange(slot_total, dtype=jnp.int32)[None, None, :]
    placing = jnp.any(select, axis=1).astype(jnp.bfloat16)
    send_tokens = jnp.einsum("ts,td->sd", placing, tokens, preferred_element_type=jnp.float32)
    send_tokens = send_tokens.astype(jnp.bfloat16).reshape(local_count, ep_ranks, CAP, quarter)
    send_grads = jnp.einsum("ts,td->sd", placing, out_grad, preferred_element_type=jnp.float32)
    send_grads = send_grads.astype(jnp.bfloat16).reshape(local_count, ep_ranks, CAP, quarter)
    send_weight = jnp.sum(
        jnp.where(select, route_weight.astype(jnp.float32)[:, :, None], 0.0), axis=(0, 1)
    )
    send_weight = send_weight.astype(jnp.bfloat16).reshape(local_count, ep_ranks, CAP)
    routed_tokens, routed_grads, routed_weight = (
        lax.all_to_all(send_tokens, "ep", split_axis=1, concat_axis=1, tiled=True),
        lax.all_to_all(send_grads, "ep", split_axis=1, concat_axis=1, tiled=True),
        lax.all_to_all(send_weight, "ep", split_axis=1, concat_axis=1, tiled=True),
    )
    routed_tokens = routed_tokens.reshape(local_count, slot_rows, quarter)
    part_gate = jnp.einsum(
        "erd,edf->erf", routed_tokens, w_gate, preferred_element_type=jnp.float32
    )
    part_up = jnp.einsum("erd,edf->erf", routed_tokens, w_up, preferred_element_type=jnp.float32)
    routed_grads = routed_grads.reshape(local_count, slot_rows, quarter)
    part_back = jnp.einsum("erd,efd->erf", routed_grads, w_down, preferred_element_type=jnp.float32)
    weight = routed_weight.reshape(local_count, slot_rows).astype(jnp.float32)
    pre_gate, pre_up, pre_back = (
        lax.psum(part_gate.astype(jnp.bfloat16), "rep").astype(jnp.float32),
        lax.psum(part_up.astype(jnp.bfloat16), "rep").astype(jnp.float32),
        lax.psum(part_back.astype(jnp.bfloat16), "rep").astype(jnp.float32),
    )
    hidden, gate_delta, up_delta = hidden_terms(pre_gate, pre_up, pre_back, weight)
    scaled_grad = (weight[:, :, None] * routed_grads.astype(jnp.float32)).astype(jnp.bfloat16)
    back_rows = jnp.einsum("erf,edf->erd", gate_delta, w_gate, preferred_element_type=jnp.float32)
    back_rows = back_rows + jnp.einsum(
        "erf,edf->erd", up_delta, w_up, preferred_element_type=jnp.float32
    )
    back_rows = back_rows.astype(jnp.bfloat16).reshape(local_count, ep_ranks, CAP, quarter)
    returned = lax.all_to_all(back_rows, "ep", split_axis=1, concat_axis=1, tiled=True)
    grad_gate = jnp.einsum(
        "erd,erf->edf", routed_tokens, gate_delta, preferred_element_type=jnp.float32
    ).astype(jnp.bfloat16)
    grad_up = jnp.einsum(
        "erd,erf->edf", routed_tokens, up_delta, preferred_element_type=jnp.float32
    ).astype(jnp.bfloat16)
    grad_down = jnp.einsum(
        "erf,erd->efd", hidden, scaled_grad, preferred_element_type=jnp.float32
    ).astype(jnp.bfloat16)
    token_grad = jnp.einsum(
        "ts,sd->td",
        placing,
        returned.reshape(slot_total, quarter),
        preferred_element_type=jnp.float32,
    )
    return (token_grad.astype(jnp.bfloat16), grad_gate, grad_up, grad_down)


def solution(mesh):
    placed = (
        P("ep", "rep"),
        P("ep", "rep"),
        P("ep", None),
        P("ep", None),
        P("ep", "rep", None),
        P("ep", "rep", None),
        P("ep", None, "rep"),
    )
    return jax.shard_map(
        body,
        mesh=mesh,
        in_specs=placed,
        out_specs=(
            P("ep", "rep"),
            P("ep", "rep", None),
            P("ep", "rep", None),
            P("ep", None, "rep"),
        ),
        check_vma=False,
    )
```

profile of v0, /device:TPU:0, one launch (start us, length us, event | category | flops | bytes accessed | tf_op | source)
XLA Modules:
  0.0 265.7 jit_solution(1522055086690203267)
XLA Ops:
  8.4 2.4 select_reduce_fusion.1
  10.9 1.5 fusion
  13.5 1.8 copy.74
  15.2 6.3 %all-to-all-start.2 = ((bf16[16,8,9,512]{3,0,2,1:T(8,128)(2,1)}), bf16[16,8,9,512]{3,0,2,1:T(8,128)(2,1)S(1)}, u32[]{:S(2)}, u32[]{:S(2)}) async-start(bf16[16,8,9,512]{3,0,2,1:T(8,128)(2,1)} %copy.74), calls=%async_computation.2 | async-start | bytes 2359296 | tf_op jit(solution)/shard_map/all_to_all | solution.py:47
  21.5 1.5 convolution_convert_fusion.4
  23.1 2.3 reshape.49
  25.4 1.8 copy.72
  27.2 23.8 %all-to-all-done.2 = bf16[16,8,9,512]{3,0,2,1:T(8,128)(2,1)S(1)} async-done(((bf16[16,8,9,512]{3,0,2,1:T(8,128)(2,1)}), bf16[16,8,9,512]{3,0,2,1:T(8,128)(2,1)S(1)}, u32[]{:S(2)}, u32[]{:S(2)}) %all-to-all-start.2) | async-done | bytes 1179680 | tf_op jit(solution)/shard_map/all_to_all | solution.py:47
  50.9 4.5 %all-to-all-start.1 = ((bf16[16,8,9,512]{3,0,2,1:T(8,128)(2,1)}), bf16[16,8,9,512]{3,0,2,1:T(8,128)(2,1)}, u32[]{:S(2)}, u32[]{:S(2)}) async-start(bf16[16,8,9,512]{3,0,2,1:T(8,128)(2,1)} %copy.72), calls=%async_computation.1 | async-start | bytes 2359296 | tf_op jit(solution)/shard_map/all_to_all | solution.py:48
  55.7 7.8 %convolution_convert_fusion.6 = bf16[16,72,640]{2,1,0:T(8,128)(2,1)} fusion(bf16[16,512,640]{2,1,0:T(8,128)(2,1)} %param.12, bf16[16,72,512]{2,0,1:T(8,128)(2,1)S(1)} %bitcast.19), kind=kOutput, calls=%fused_computation.26 | convolution fusion | flops 755712000 | bytes 13139968 | tf_op jit(solution)/shard_map/erd,edf->erf/dot_general | solution.py:55
  63.5 3.6 %convolution_convert_fusion.5 = bf16[16,72,640]{2,1,0:T(8,128)(2,1)} fusion(bf16[16,512,640]{2,1,0:T(8,128)(2,1)S(1)} %bitcast.16, bf16[16,72,512]{2,0,1:T(8,128)(2,1)S(1)} %bitcast.20), kind=kOutput, calls=%fused_computation.25 | convolution fusion | flops 755712000 | bytes 13139968 | tf_op jit(solution)/shard_map/erd,edf->erf/dot_general | solution.py:52
  67.2 17.7 %all-to-all-done.1 = bf16[16,8,9,512]{3,0,2,1:T(8,128)(2,1)} async-done(((bf16[16,8,9,512]{3,0,2,1:T(8,128)(2,1)}), bf16[16,8,9,512]{3,0,2,1:T(8,128)(2,1)}, u32[]{:S(2)}, u32[]{:S(2)}) %all-to-all-start.1) | async-done | bytes 1179680 | tf_op jit(solution)/shard_map/all_to_all | solution.py:48
  84.9 8.8 %convolution_convert_fusion.7 = bf16[16,72,640]{2,1,0:T(8,128)(2,1)} fusion(bf16[16,640,512]{2,1,0:T(8,128)(2,1)} %param.13, bf16[16,72,512]{2,0,1:T(8,128)(2,1)} %bitcast), kind=kOutput, calls=%fused_computation.27 | convolution fusion | flops 755712000 | bytes 13139968 | tf_op jit(solution)/shard_map/erd,efd->erf/dot_general | solution.py:57
  95.4 8.1 %all_to_all.20 = bf16[16,8,9]{2,0,1:T(8,128)(2,1)S(1)} all-to-all(bf16[16,8,9]{2,0,1:T(8,128)(2,1)S(1)} %copy.69), channel_id=1, replica_groups=mesh['rep'=4,'ep'=8] {'ep'}, dimensions={1} | all-to-all | bytes 4608 | tf_op jit(solution)/shard_map/all_to_all | solution.py:49
  104.0 2.9 %multiply_convert_fusion.1 = bf16[16,72,512]{2,0,1:T(8,128)(2,1)} fusion(f32[16,72]{0,1:T(8,128)S(1)} %copy.81, bf16[16,8,9,512]{3,0,2,1:T(8,128)(2,1)} %all-to-all-done.1), kind=kLoop, calls=%fused_computation.23 | loop fusion | flops 1769472 | bytes 2363904 | tf_op jit(solution)/shard_map/convert_element_type | solution.py:65
  106.9 94.3 %all-reduce.3.cloned.1.call-done = (bf16[16,72,640]{2,1,0:T(8,128)(2,1)}, bf16[16,72,640]{2,1,0:T(8,128)(2,1)}, bf16[16,72,640]{2,1,0:T(8,128)(2,1)}) async-done(((bf16[16,72,640]{2,1,0:T(8,128)(2,1)}, bf16[16,72,640]{2,1,0:T(8,128)(2,1)}, bf16[16,72,640]{2,1,0:T(8,128)(2,1)}), (bf16[16,72,640]{2,1,0:T(8,128)(2,1)}, bf16[16,72,640]{2,1,0:T(8,128)(2,1)}, ...) | async-done | bytes 4423696 | tf_op jit(solution)/shard_map/psum | solution.py:61
  201.2 10.8 %fusion.26 = f32[16,72,512]{2,1,0:T(8,128)} fusion(bf16[16,512,640]{2,1,0:T(8,128)(2,1)} %param.11, bf16[16,72,640]{2,1,0:T(8,128)(2,1)} %get-tuple-element.4, bf16[16,72,640]{2,1,0:T(8,128)(2,1)} %get-tuple-element.5, bf16[16,72,640]{2,1,0:T(8,128)(2,1)} %get-tuple-element.6, f32[16,72]{1,0:T(8,128)S(1)} %reshape.55), kind=kOutput, calls=%fused_computation.53 | convolution fusion | flops 765296640 | bytes 17273344 | tf_op jit(solution)/shard_map/erf,edf->erd/dot_general | solution.py:66
  212.0 7.7 %add_convert_fusion = bf16[16,72,512]{2,1,0:T(8,128)(2,1)} fusion(f32[16,72,512]{2,1,0:T(8,128)} %fusion.26, bf16[16,512,640]{2,1,0:T(8,128)(2,1)S(1)} %bitcast.18, bf16[16,72,640]{2,1,0:T(8,128)(2,1)} %get-tuple-element.6, f32[16,72]{1,0:T(8,128)S(1)} %reshape.55, bf16[16,72,640]{2,1,0:T(8,128)(2,1)} %get-tuple-element.5), kind=kOutput, calls=%fused_computation.24 | convolution fusion | flops 762789888 | bytes 16978432 | tf_op jit(solution)/shard_map/erf,edf->erd/dot_general | solution.py:67
  219.7 2.7 %copy.77 = bf16[16,72,512]{2,0,1:T(8,128)(2,1)} copy(bf16[16,72,512]{2,1,0:T(8,128)(2,1)} %add_convert_fusion) | data formatting | bytes 2359296 | tf_op jit(solution)/shard_map/convert_element_type | solution.py:70
  222.5 4.6 %all-to-all-start.3 = ((bf16[16,8,9,512]{3,0,2,1:T(8,128)(2,1)}), bf16[16,8,9,512]{3,0,2,1:T(8,128)(2,1)S(1)}, u32[]{:S(2)}, u32[]{:S(2)}) async-start(bf16[16,8,9,512]{3,0,2,1:T(8,128)(2,1)} %bitcast.2), calls=%async_computation.3 | async-start | bytes 2359296 | tf_op jit(solution)/shard_map/all_to_all | solution.py:71
  227.1 7.9 %convolution_convert_fusion = bf16[16,640,512]{2,1,0:T(8,128)(2,1)} fusion(bf16[16,72,640]{2,1,0:T(8,128)(2,1)} %get-tuple-element.4, bf16[16,72,640]{2,1,0:T(8,128)(2,1)} %get-tuple-element.5, bf16[16,72,512]{2,0,1:T(8,128)(2,1)S(1)} %copy-done.4), kind=kOutput, calls=%fused_computation | convolution fusion | flops 766115840 | bytes 14614528 | tf_op jit(solution)/shard_map/erf,erd->efd/dot_general | solution.py:78
  235.0 6.5 %convolution_convert_fusion.1 = bf16[16,512,640]{2,1,0:T(8,128)(2,1)} fusion(bf16[16,72,512]{2,0,1:T(8,128)(2,1)S(1)} %bitcast.21, bf16[16,72,640]{2,1,0:T(8,128)(2,1)S(1)} %copy-done.11, f32[16,72]{1,0:T(8,128)S(1)} %reshape.55, bf16[16,72,640]{2,1,0:T(8,128)(2,1)S(1)} %copy-done.10), kind=kOutput, calls=%fused_computation.1 | convolution fusion | flops 766853120 | bytes 14619136 | tf_op jit(solution)/shard_map/erd,erf->edf/dot_general | solution.py:75
  241.6 7.2 %convolution_convert_fusion.2 = bf16[16,512,640]{2,1,0:T(8,128)(2,1)} fusion(bf16[16,72,512]{2,0,1:T(8,128)(2,1)S(1)} %bitcast.22, bf16[16,72,640]{2,1,0:T(8,128)(2,1)S(1)} %copy-done.9, bf16[16,72,640]{2,1,0:T(8,128)(2,1)S(1)} %copy-done.10, bf16[16,72,640]{2,1,0:T(8,128)(2,1)S(1)} %copy-done.11, f32[16,72]{1,0:T(8,128)S(1)} %reshape.55), kind=kOutput, calls=%fused_computation.2 | convolution fusion | flops 770539520 | bytes 16093696 | tf_op jit(solution)/shard_map/erd,erf->edf/dot_general | solution.py:72
  248.8 7.7 %all-to-all-done.3 = bf16[16,8,9,512]{3,0,2,1:T(8,128)(2,1)S(1)} async-done(((bf16[16,8,9,512]{3,0,2,1:T(8,128)(2,1)}), bf16[16,8,9,512]{3,0,2,1:T(8,128)(2,1)S(1)}, u32[]{:S(2)}, u32[]{:S(2)}) %all-to-all-start.3) | async-done | bytes 1179680 | tf_op jit(solution)/shard_map/all_to_all | solution.py:71
  (58 shorter events, 7.1 us)
Async XLA Ops:
  7.2 5.2 %copy-start = (bf16[128,512]{1,0:T(8,128)(2,1)S(1)}, bf16[128,512]{1,0:T(8,128)(2,1)}, u32[]{:S(2)}) copy-start(bf16[128,512]{1,0:T(8,128)(2,1)} %param.7) | copy-start | bytes 393220
  10.9 1.5 copy-start.5
  13.4 8.1 %copy-start.7 = (bf16[128,512]{1,0:T(8,128)(2,1)S(1)}, bf16[128,512]{1,0:T(8,128)(2,1)}, u32[]{:S(2)}) copy-start(bf16[128,512]{1,0:T(8,128)(2,1)} %param.8) | copy-start | bytes 393220
  15.2 35.7 %all-to-all-start.2 = ((bf16[16,8,9,512]{3,0,2,1:T(8,128)(2,1)}), bf16[16,8,9,512]{3,0,2,1:T(8,128)(2,1)S(1)}, u32[]{:S(2)}, u32[]{:S(2)}) async-start(bf16[16,8,9,512]{3,0,2,1:T(8,128)(2,1)} %copy.74), calls=%async_computation.2 | async-start | bytes 2359296 | tf_op jit(solution)/shard_map/all_to_all | solution.py:47
  50.9 12.6 %copy-start.2 = (bf16[16,8,9,512]{3,0,2,1:T(8,128)(2,1)}, bf16[16,8,9,512]{3,0,2,1:T(8,128)(2,1)S(1)}, u32[]{:S(2)}) copy-start(bf16[16,8,9,512]{3,0,2,1:T(8,128)(2,1)S(1)} %all-to-all-done.2) | copy-start | bytes 3538948
  50.9 12.6 %slice-start = ((s8[10485760]{0:T(1024)(128)(4,1)}), s8[2097152]{0:T(1024)(128)(4,1)S(1)}, s32[]{:S(2)}) async-start(s8[10485760]{0:T(1024)(128)(4,1)} %bitcast.15), calls=%async_computation.5 | async-start | bytes 4194304
  50.9 33.9 %all-to-all-start.1 = ((bf16[16,8,9,512]{3,0,2,1:T(8,128)(2,1)}), bf16[16,8,9,512]{3,0,2,1:T(8,128)(2,1)}, u32[]{:S(2)}, u32[]{:S(2)}) async-start(bf16[16,8,9,512]{3,0,2,1:T(8,128)(2,1)} %copy.72), calls=%async_computation.1 | async-start | bytes 2359296 | tf_op jit(solution)/shard_map/all_to_all | solution.py:48
  55.5 145.7 %all-reduce.3.cloned.1.call-start = ((), (), s32[]{:S(2)}) async-start(), calls=%async_computation.4 | async-start | bytes 8847360 | tf_op jit(solution)/shard_map/psum | solution.py:61
  55.7 7.8 %slice-start.1 = ((s8[10485760]{0:T(1024)(128)(4,1)}), s8[4194304]{0:T(1024)(128)(4,1)S(1)}, s32[]{:S(2)}) async-start(s8[10485760]{0:T(1024)(128)(4,1)} %bitcast.15), calls=%async_computation.6 | async-start | bytes 8388608
  55.7 7.8 %slice-start.2 = ((s8[10485760]{0:T(1024)(128)(4,1)}), s8[4194304]{0:T(1024)(128)(4,1)S(1)}, s32[]{:S(2)}) async-start(s8[10485760]{0:T(1024)(128)(4,1)} %bitcast.15), calls=%async_computation.7 | async-start | bytes 8388608
  93.7 0.7 copy-start.8
  93.7 0.9 copy-start.6
  103.9 108.1 %slice-start.3 = ((s8[10485760]{0:T(1024)(128)(4,1)}), s8[2097152]{0:T(1024)(128)(4,1)S(1)}, s32[]{:S(2)}) async-start(s8[10485760]{0:T(1024)(128)(4,1)} %bitcast.17), calls=%async_computation.8 | async-start | bytes 4194304
  201.2 10.8 %slice-start.4 = ((s8[10485760]{0:T(1024)(128)(4,1)}), s8[4194304]{0:T(1024)(128)(4,1)S(1)}, s32[]{:S(2)}) async-start(s8[10485760]{0:T(1024)(128)(4,1)} %bitcast.17), calls=%async_computation.9 | async-start | bytes 8388608
  201.2 10.8 %slice-start.5 = ((s8[10485760]{0:T(1024)(128)(4,1)}), s8[4194304]{0:T(1024)(128)(4,1)S(1)}, s32[]{:S(2)}) async-start(s8[10485760]{0:T(1024)(128)(4,1)} %bitcast.17), calls=%async_computation.10 | async-start | bytes 8388608
  219.7 7.4 %copy-start.4 = (bf16[16,72,512]{2,0,1:T(8,128)(2,1)S(1)}, bf16[16,72,512]{2,0,1:T(8,128)(2,1)}, u32[]{:S(2)}) copy-start(bf16[16,72,512]{2,0,1:T(8,128)(2,1)} %multiply_convert_fusion.1) | copy-start | bytes 3538948
  222.5 34.0 %all-to-all-start.3 = ((bf16[16,8,9,512]{3,0,2,1:T(8,128)(2,1)}), bf16[16,8,9,512]{3,0,2,1:T(8,128)(2,1)S(1)}, u32[]{:S(2)}, u32[]{:S(2)}) async-start(bf16[16,8,9,512]{3,0,2,1:T(8,128)(2,1)} %bitcast.2), calls=%async_computation.3 | async-start | bytes 2359296 | tf_op jit(solution)/shard_map/all_to_all | solution.py:71
  227.1 7.9 %copy-start.3 = (bf16[16,8,9,512]{3,0,2,1:T(8,128)(2,1)S(1)}, bf16[16,8,9,512]{3,0,2,1:T(8,128)(2,1)}, u32[]{:S(2)}) copy-start(bf16[16,8,9,512]{3,0,2,1:T(8,128)(2,1)} %copy-done.2) | copy-start | bytes 3538948
  227.1 7.9 %copy-start.10 = (bf16[16,72,640]{2,1,0:T(8,128)(2,1)S(1)}, bf16[16,72,640]{2,1,0:T(8,128)(2,1)}, u32[]{:S(2)}) copy-start(bf16[16,72,640]{2,1,0:T(8,128)(2,1)} %get-tuple-element.5) | copy-start | bytes 4423684
  227.1 7.9 %copy-start.11 = (bf16[16,72,640]{2,1,0:T(8,128)(2,1)S(1)}, bf16[16,72,640]{2,1,0:T(8,128)(2,1)}, u32[]{:S(2)}) copy-start(bf16[16,72,640]{2,1,0:T(8,128)(2,1)} %get-tuple-element.6) | copy-start | bytes 4423684
  235.0 6.5 %copy-start.9 = (bf16[16,72,640]{2,1,0:T(8,128)(2,1)S(1)}, bf16[16,72,640]{2,1,0:T(8,128)(2,1)}, u32[]{:S(2)}) copy-start(bf16[16,72,640]{2,1,0:T(8,128)(2,1)} %get-tuple-element.4) | copy-start | bytes 4423684
  256.5 2.3 copy-start.1
Sparse Core Ops, SparseCore 0:
  93.8 107.3 all-reduce.2
where the time goes:
time: 266 us
  waiting for transfers between devices  144 us (54%)
  matrix products  63.4 us (24%)
  starting transfers between devices  15.7 us (6%)
  between operations  14.3 us (5%)
  local copies, waits for them, and re-layouts  12.8 us (5%)
  blocking collectives  8.12 us (3%)
  other arithmetic  7.89 us (3%)
    psum x1, waiting for transfers between devices, body(): lax.psum(part_up.astype(jnp.bfloat16), 'rep').astype(jnp.float32)  94.3 us
    all_to_all x1, waiting for transfers between devices, body(): lax.all_to_all(send_tokens, 'ep', split_axis=1, concat_axis=1, tiled=True)  23.8 us
    all_to_all x1, waiting for transfers between devices, body(): lax.all_to_all(send_grads, 'ep', split_axis=1, concat_axis=1, tiled=True)  17.7 us
    dot_general x1, matrix products, body(): jnp.einsum('erf,edf->erd', gate_delta, w_gate, preferred_element_type=jnp...  10.8 us
    dot_general x1, matrix products, body(): jnp.einsum('erd,efd->erf', routed_grads, w_down, preferred_element_type=j...  8.78 us
    all_to_all x1, blocking collectives, body(): lax.all_to_all(send_weight, 'ep', split_axis=1, concat_axis=1, tiled=True)  8.12 us
    dot_general x1, matrix products, body(): jnp.einsum('erf,erd->efd', hidden, scaled_grad, preferred_element_type=jn...  7.89 us
    dot_general x1, matrix products, body(): jnp.einsum('erd,edf->erf', routed_tokens, w_up, preferred_element_type=jn...  7.76 us
  transfers between devices with their start and end apart: 4, of which 4 were waited for; matrix products, arithmetic and copies ran while one was open for 16% of the time, Pallas kernels for 0%

commit v1 on v0

--- a/solution.py
+++ b/solution.py
@@ -1,6 +1,8 @@
 import jax
 import jax.numpy as jnp
 from jax import lax
+from jax.experimental import pallas as pl
+from jax.experimental.pallas import tpu as pltpu
 from jax.sharding import PartitionSpec as P
 
 CAP = 9
@@ -87,6 +89,202 @@
     return (token_grad.astype(jnp.bfloat16), grad_gate, grad_up, grad_down)
 
 
+def routes(slot_row, slot_rows):
+    rows = lax.broadcasted_iota(jnp.int32, (slot_rows, slot_row.shape[1]), 0)
+    return rows == slot_row
+
+
+def pre_kernel(slot_ref, tok_ref, wg_ref, wu_ref, wd_ref, *rest):
+    rows_ref, part_ref = rest[-2:]
+    slot_rows = rows_ref.shape[1]
+    half = wg_ref.shape[1]
+    ffw = wg_ref.shape[2]
+    place = routes(slot_ref[0], slot_rows).astype(jnp.bfloat16)
+    rows = jnp.dot(place, tok_ref[...], preferred_element_type=jnp.float32).astype(jnp.bfloat16)
+    rows_ref[0] = rows
+    gate = jnp.dot(rows[:, :half], wg_ref[0], preferred_element_type=jnp.float32)
+    part_ref[0, :, :ffw] = gate.astype(jnp.bfloat16)
+    up = jnp.dot(rows[:, :half], wu_ref[0], preferred_element_type=jnp.float32)
+    part_ref[0, :, ffw : 2 * ffw] = up.astype(jnp.bfloat16)
+    back = lax.dot_general(
+        rows[:, half:], wd_ref[0], (((1,), (1,)), ((), ())), preferred_element_type=jnp.float32
+    )
+    part_ref[0, :, 2 * ffw :] = back.astype(jnp.bfloat16)
+
+
+def post_kernel(slot_ref, weight_ref, rows_ref, sum_ref, wg_ref, wu_ref, *rest):
+    acc_in, total_ref, gg_ref, gu_ref, gd_ref = rest[0], *rest[-4:]
+    slot_rows = rows_ref.shape[1]
+    half = wg_ref.shape[1]
+    ffw = wg_ref.shape[2]
+    hit = routes(slot_ref[0], slot_rows)
+    weight = jnp.sum(jnp.where(hit, weight_ref[0], 0.0), axis=1, keepdims=True)
+    place = hit.astype(jnp.bfloat16)
+    pre_gate = sum_ref[0, :, :ffw].astype(jnp.float32)
+    pre_up = sum_ref[0, :, ffw : 2 * ffw].astype(jnp.float32)
+    pre_back = sum_ref[0, :, 2 * ffw :].astype(jnp.float32)
+    sig = jax.nn.sigmoid(pre_gate)
+    silu = pre_gate * sig
+    d_hidden = weight * pre_back
+    hidden = (silu * pre_up).astype(jnp.bfloat16)
+    gate_delta = (d_hidden * pre_up * sig * (1.0 + pre_gate * (1.0 - sig))).astype(jnp.bfloat16)
+    up_delta = (d_hidden * silu).astype(jnp.bfloat16)
+    rows_in = rows_ref[0, :, :half]
+    scaled = (weight * rows_ref[0, :, half:].astype(jnp.float32)).astype(jnp.bfloat16)
+    nt = (((1,), (1,)), ((), ()))
+    tn = (((0,), (0,)), ((), ()))
+    f32 = jnp.float32
+    back = lax.dot_general(gate_delta, wg_ref[0], nt, preferred_element_type=f32)
+    back = back + lax.dot_general(up_delta, wu_ref[0], nt, preferred_element_type=f32)
+    gg_ref[0] = lax.dot_general(rows_in, gate_delta, tn, preferred_element_type=f32).astype(
+        jnp.bfloat16
+    )
+    gu_ref[0] = lax.dot_general(rows_in, up_delta, tn, preferred_element_type=f32).astype(
+        jnp.bfloat16
+    )
+    gd_ref[0] = lax.dot_general(hidden, scaled, tn, preferred_element_type=f32).astype(jnp.bfloat16)
+
+    @pl.when(pl.program_id(0) == 0)
+    def _():
+        total_ref[...] = acc_in[...]
+
+    total_ref[...] += lax.dot_general(
+        place, back.astype(jnp.bfloat16), tn, preferred_element_type=f32
+    )
+
+
+def pre_call(first, count, slot, gathered, w_gate, w_up, w_down, slot_rows, after):
+    quarter, ffw = w_gate.shape[1:]
+    token_count = slot.shape[2]
+    mine = lambda i: (first + i, 0, 0)
+    local = lambda i: (i, 0, 0)
+    flops = 2 * count * slot_rows * quarter * (2 * token_count + 3 * ffw)
+    return pl.pallas_call(
+        pre_kernel,
+        grid=(count,),
+        in_specs=[
+            pl.BlockSpec((1, 1, token_count), mine),
+            pl.BlockSpec((token_count, 2 * quarter), lambda i: (0, 0)),
+            pl.BlockSpec((1, quarter, ffw), mine),
+            pl.BlockSpec((1, quarter, ffw), mine),
+            pl.BlockSpec((1, ffw, quarter), mine),
+        ]
+        + [pl.BlockSpec(memory_space=pl.ANY)] * len(after),
+        out_specs=[
+            pl.BlockSpec((1, slot_rows, 2 * quarter), local),
+            pl.BlockSpec((1, slot_rows, 3 * ffw), local),
+        ],
+        out_shape=[
+            jax.ShapeDtypeStruct((count, slot_rows, 2 * quarter), jnp.bfloat16),
+            jax.ShapeDtypeStruct((count, slot_rows, 3 * ffw), jnp.bfloat16),
+        ],
+        compiler_params=pltpu.CompilerParams(vmem_limit_bytes=32 << 20),
+        cost_estimate=pl.CostEstimate(
+            flops=flops, bytes_accessed=count * 6 * quarter * ffw, transcendentals=0
+        ),
+    )(slot, gathered, w_gate, w_up, w_down, *after)
+
+
+def post_call(first, count, slot, weight, rows, summed, w_gate, w_up, total, grads):
+    quarter, ffw = w_gate.shape[1:]
+    local_count = w_gate.shape[0]
+    token_count = slot.shape[2]
+    slot_rows = rows.shape[1]
+    mine = lambda i: (first + i, 0, 0)
+    local = lambda i: (i, 0, 0)
+    whole = lambda i: (0, 0)
+    up_shape = jax.ShapeDtypeStruct((local_count, quarter, ffw), jnp.bfloat16)
+    down_shape = jax.ShapeDtypeStruct((local_count, ffw, quarter), jnp.bfloat16)
+    return pl.pallas_call(
+        post_kernel,
+        grid=(count,),
+        in_specs=[
+            pl.BlockSpec((1, 1, token_count), mine),
+            pl.BlockSpec((1, 1, token_count), mine),
+            pl.BlockSpec((1, slot_rows, 2 * quarter), local),
+            pl.BlockSpec((1, slot_rows, 3 * ffw), local),
+            pl.BlockSpec((1, quarter, ffw), mine),
+            pl.BlockSpec((1, quarter, ffw), mine),
+            pl.BlockSpec((token_count, quarter), whole),
+        ]
+        + [pl.BlockSpec(memory_space=pl.ANY)] * len(grads),
+        out_specs=[
+            pl.BlockSpec((token_count, quarter), whole),
+            pl.BlockSpec((1, quarter, ffw), mine),
+            pl.BlockSpec((1, quarter, ffw), mine),
+            pl.BlockSpec((1, ffw, quarter), mine),
+        ],
+        out_shape=[
+            jax.ShapeDtypeStruct((token_count, quarter), jnp.float32),
+            up_shape,
+            up_shape,
+            down_shape,
+        ],
+        input_output_aliases={7 + i: 1 + i for i in range(len(grads))},
+        compiler_params=pltpu.CompilerParams(vmem_limit_bytes=40 << 20),
+        cost_estimate=pl.CostEstimate(
+            flops=2 * count * slot_rows * quarter * (5 * ffw + token_count),
+            bytes_accessed=count * 10 * quarter * ffw,
+            transcendentals=0,
+        ),
+    )(slot, weight, rows, summed, w_gate, w_up, total, *grads)
+
+
+CHUNKS = 4
+LAG = 1
+
+
+def gathered_body(tokens, out_grad, expert_ids, route_weight, w_gate, w_up, w_down):
+    ep_ranks = lax.axis_size("ep")
+    local_count, quarter, ffw = w_gate.shape
+    experts = local_count * ep_ranks
+    slot_rows = ep_ranks * CAP
+    rows, picks = expert_ids.shape
+    matches = expert_ids[:, :, None] == jnp.arange(experts, dtype=jnp.int32)[None, None, :]
+    picked = jnp.sum(matches.astype(jnp.float32), axis=1).astype(jnp.bfloat16)
+    earlier = jnp.tril(jnp.ones((rows, rows), jnp.bfloat16), -1)
+    before = jnp.dot(earlier, picked, preferred_element_type=jnp.float32)
+    position = jnp.sum(jnp.where(matches, before[:, None, :], 0.0), axis=2)
+    facts = jnp.concatenate(
+        [expert_ids.astype(jnp.bfloat16), position.astype(jnp.bfloat16), route_weight]
+        + [jnp.zeros((rows, 128 - 3 * picks), jnp.bfloat16)],
+        axis=1,
+    )
+    packed = jnp.concatenate([tokens, out_grad, facts], axis=1)
+    everyone = lax.all_gather(packed, "ep", axis=0, tiled=True)
+    token_count = rows * ep_ranks
+    facts = everyone[:, 2 * quarter : 2 * quarter + 3 * picks].astype(jnp.float32).T
+    column = (jnp.arange(token_count, dtype=jnp.int32) // rows).astype(jnp.float32)
+    first = lax.axis_index("ep") * local_count
+    mine = (first + jnp.arange(local_count, dtype=jnp.int32)).astype(jnp.float32)[:, None]
+    slot = jnp.full((local_count, token_count), -1.0, jnp.float32)
+    weight = jnp.zeros((local_count, token_count), jnp.float32)
+    for k in range(picks):
+        here = facts[k][None, :] == mine
+        slot = jnp.where(here, (column * CAP + facts[picks + k])[None, :], slot)
+        weight = jnp.where(here, facts[2 * picks + k][None, :], weight)
+    slot = slot.astype(jnp.int32)[:, None, :]
+    weight = weight[:, None, :]
+    count = local_count // CHUNKS
+    summed, routed = [], []
+    for c in range(CHUNKS):
+        after = summed[c - LAG : c - LAG + 1] if c >= LAG else []
+        got, part = pre_call(
+            c * count, count, slot, everyone, w_gate, w_up, w_down, slot_rows, after
+        )
+        routed.append(got)
+        summed.append(lax.psum(part, "rep"))
+    total, grads = jnp.zeros((token_count, quarter), jnp.float32), []
+    for c in range(CHUNKS):
+        total, *grads = post_call(
+            c * count, count, slot, weight, routed[c], summed[c], w_gate, w_up, total, grads
+        )
+    token_grad = lax.psum_scatter(
+        total.astype(jnp.bfloat16), "ep", scatter_dimension=0, tiled=True
+    )
+    return (token_grad, *grads)
+
+
 def solution(mesh):
     placed = (
         P("ep", "rep"),
@@ -98,7 +296,7 @@
         P("ep", None, "rep"),
     )
     return jax.shard_map(
-        body,
+        gathered_body if mesh.shape["ep"] <= 8 else body,
         mesh=mesh,
         in_specs=placed,
         out_specs=(

time: 266 us -> 365 us (1.37)
  waiting for transfers between devices: 144 us -> 252 us
  matrix products: 63.4 us -> 0.2 us
  Pallas kernels: 0 us -> 57.5 us
  starting transfers between devices: 15.7 us -> 0.43 us
  local copies, waits for them, and re-layouts: 12.8 us -> 27.6 us
  blocking collectives: 8.12 us -> 0 us
  other arithmetic: 7.89 us -> 12.1 us
    psum x1 -> x4, waiting for transfers between devices: 94.3 us -> 185 us  [gathered_body(): summed.append(lax.psum(part, 'rep'))]
    dot_general x11 -> x1, matrix products: 63.4 us -> 0.2 us  [gathered_body(): before = jnp.dot(earlier, picked, preferred_element_type=jnp.float32)]
    pallas_call x0 -> x8, Pallas kernels: none -> 57.5 us  [the longest x4 34.4 us: post_call(): pl.pallas_call(post_kernel, grid=(count,), in_specs=[pl.BlockSpec((1, 1,...]
    all_to_all x3 -> x0, waiting for transfers between devices: 49.2 us -> none  [the longest x1 23.8 us: body(): lax.all_to_all(send_tokens, 'ep', split_axis=1, concat_axis=1, tiled=True)]
    all_gather x0 -> x1, waiting for transfers between devices: none -> 34.4 us  [gathered_body(): everyone = lax.all_gather(packed, 'ep', axis=0, tiled=True)]
    reduce_scatter x0 -> x1, waiting for transfers between devices: none -> 32.5 us  [gathered_body(): lax.psum_scatter(total.astype(jnp.bfloat16), 'ep', scatter_dimension=0, t...]
    unnamed x37 -> x52, local copies, waits for them, and re-layouts: 1.62 us -> 25.5 us
    all_to_all x3 -> x0, starting transfers between devices: 15.5 us -> none  [the longest x1 6.32 us: body(): lax.all_to_all(send_tokens, 'ep', split_axis=1, concat_axis=1, tiled=True)]
  transfers between devices with their start and end apart: 4 -> 6, of which waited for: 4 -> 6; matrix products, arithmetic and copies ran while one was open for 16% -> 0% of each run, Pallas kernels for 0% -> 7%
where the time goes in v1:
time: 365 us; the launch traced here: 364 us
  waiting for transfers between devices  252 us (69%)
  Pallas kernels  57.5 us (16%)
  local copies, waits for them, and re-layouts  27.6 us (8%)
  between operations  14.3 us (4%)
  other arithmetic  12.1 us (3%)
    psum x4, waiting for transfers between devices, gathered_body(): summed.append(lax.psum(part, 'rep'))  185 us
    pallas_call x4, Pallas kernels, post_call(): pl.pallas_call(post_kernel, grid=(count,), in_specs=[pl.BlockSpec((1, 1,...  34.4 us
    all_gather x1, waiting for transfers between devices, gathered_body(): everyone = lax.all_gather(packed, 'ep', axis=0, tiled=True)  34.4 us
    reduce_scatter x1, waiting for transfers between devices, gathered_body(): lax.psum_scatter(total.astype(jnp.bfloat16), 'ep', scatter_dimension=0, t...  32.5 us
    unnamed x52, local copies, waits for them, and re-layouts  25.5 us
    pallas_call x4, Pallas kernels, pre_call(): pl.pallas_call(pre_kernel, grid=(count,), in_specs=[pl.BlockSpec((1, 1, t...  23.1 us
  transfers between devices with their start and end apart: 6, of which 6 were waited for; matrix products, arithmetic and copies ran while one was open for 0% of the time, Pallas kernels for 7%

profile of v1, /device:TPU:0, one launch (start us, length us, event | category | flops | bytes accessed | tf_op | source)
XLA Modules:
  0.0 363.9 jit_solution(10179771535235723894)
XLA Ops:
  10.5 1.8 concatenate.3
  12.4 34.4 %all-gather.2.cloned.1.call-done.tok_ref = bf16[1024,1152]{1,0:T(8,128)(2,1)} async-done(((bf16[128,1152]{1,0:T(8,128)(2,1)}), bf16[1024,1152]{1,0:T(8,128)(2,1)}) %all-gather.2.cloned.1.call-update) | async-done | bytes 2359312 | tf_op jit(solution)/shard_map/all_gather | solution.py:254
  47.9 5.6 %slice_reduce_fusion.7 = (f32[1024]{0:T(1024)}, f32[1024]{0:T(1024)}, f32[1024]{0:T(1024)}, f32[1024]{0:T(1024)}, f32[1024]{0:T(1024)}, /*index=5*/f32[1024]{0:T...) fusion(f32[24,1024]{0,1:T(8,128)S(1)} %convert_bitcast_fusion), kind=kLoop, calls=%fused_computation.31 | loop fusion | flops 16384 | bytes 155648 | tf_op jit(solution)/shard_map/slice | solution.py:265
  53.5 1.4 slice_reduce_fusion.15
  55.9 6.2 %shard_map.102 = (bf16[4,72,1024]{2,1,0:T(8,128)(2,1)S(1)}, bf16[4,72,1920]{2,1,0:T(8,128)(2,1)}) custom-call(s32[16,1,1024]{2,1,0:T(1,128)S(1)} %fusion.21.slot_ref, bf16[1024,1152]{1,0:T(8,128)(2,1)S(1)} %copy-done.4, bf16[16,512,640]{2,1,0:T(8,128)(2,1)S(1)} %copy-done, bf16[16,512,640]{2,1,0:T(8,128)(2,1)} %wu_ref.15, bf16[16,640,512]{2,1,0:T(8,128)(2,1)} %wd_ref.7), custom_call_target="tpu_custom_call" | custom-call | flops 1170210816 | bytes 7864320 | tf_op jit(solution)/shard_map/pallas_call | solution.py:162
  63.0 52.6 %all-reduce.5.cloned.1.call-done.rest_0_.sum_ref = bf16[4,72,1920]{2,1,0:T(8,128)(2,1)} async-done(((bf16[4,72,1920]{2,1,0:T(8,128)(2,1)}), bf16[4,72,1920]{2,1,0:T(8,128)(2,1)}) %all-reduce.5.cloned.1.call-update) | async-done | bytes 1105936 | tf_op jit(solution)/shard_map/psum | solution.py:276
  115.6 4.0 %copy-done.1 = bf16[16,512,640]{2,1,0:T(8,128)(2,1)S(1)} copy-done((bf16[16,512,640]{2,1,0:T(8,128)(2,1)S(1)}, bf16[16,512,640]{2,1,0:T(8,128)(2,1)}, u32[]{:S(2)}) %copy-start.1) | copy-done | bytes 10485784
  119.6 1.2 copy-done.9
  120.8 6.2 %shard_map.103 = (bf16[4,72,1024]{2,1,0:T(8,128)(2,1)S(1)}, bf16[4,72,1920]{2,1,0:T(8,128)(2,1)}) custom-call(s32[16,1,1024]{2,1,0:T(1,128)S(1)} %fusion.21.slot_ref, bf16[1024,1152]{1,0:T(8,128)(2,1)S(1)} %copy-done.4, bf16[16,512,640]{2,1,0:T(8,128)(2,1)S(1)} %copy-done.1, bf16[16,512,640]{2,1,0:T(8,128)(2,1)} %wu_ref.15, bf16[16,640,512]{2,1,0:T(8,128)(2,1)} %wd_ref.7, ...), custom_call_target="tpu_custom_call" | custom-call | flops 1170210816 | bytes 7864320 | tf_op jit(solution)/shard_map/pallas_call | solution.py:162
  127.9 53.6 %all-reduce.7.cloned.1.call-done.rest_0_.sum_ref = bf16[4,72,1920]{2,1,0:T(8,128)(2,1)} async-done(((bf16[4,72,1920]{2,1,0:T(8,128)(2,1)}), bf16[4,72,1920]{2,1,0:T(8,128)(2,1)}) %all-reduce.7.cloned.1.call-update) | async-done | bytes 1105936 | tf_op jit(solution)/shard_map/psum | solution.py:276
  181.5 4.0 %copy-done.2 = bf16[16,512,640]{2,1,0:T(8,128)(2,1)S(1)} copy-done((bf16[16,512,640]{2,1,0:T(8,128)(2,1)S(1)}, bf16[16,512,640]{2,1,0:T(8,128)(2,1)}, u32[]{:S(2)}) %copy-start.2) | copy-done | bytes 10485784
  185.5 1.2 copy-done.5
  186.7 5.3 %shard_map.104 = (bf16[4,72,1024]{2,1,0:T(8,128)(2,1)S(1)}, bf16[4,72,1920]{2,1,0:T(8,128)(2,1)S(1)}) custom-call(s32[16,1,1024]{2,1,0:T(1,128)S(1)} %fusion.21.slot_ref, bf16[1024,1152]{1,0:T(8,128)(2,1)S(1)} %copy-done.4, bf16[16,512,640]{2,1,0:T(8,128)(2,1)S(1)} %copy-done.2, bf16[16,512,640]{2,1,0:T(8,128)(2,1)} %wu_ref.15, ...), custom_call_target="tpu_custom_call" | custom-call | flops 1170210816 | bytes 7864320 | tf_op jit(solution)/shard_map/pallas_call | solution.py:162
  194.0 53.6 %all-reduce.9.cloned.1.call-done.rest_0_.sum_ref = bf16[4,72,1920]{2,1,0:T(8,128)(2,1)} async-done(((bf16[4,72,1920]{2,1,0:T(8,128)(2,1)}), bf16[4,72,1920]{2,1,0:T(8,128)(2,1)}) %all-reduce.9.cloned.1.call-update) | async-done | bytes 1105936 | tf_op jit(solution)/shard_map/psum | solution.py:276
  247.5 4.0 %copy-done.3 = bf16[16,512,640]{2,1,0:T(8,128)(2,1)S(1)} copy-done((bf16[16,512,640]{2,1,0:T(8,128)(2,1)S(1)}, bf16[16,512,640]{2,1,0:T(8,128)(2,1)}, u32[]{:S(2)}) %copy-start.3) | copy-done | bytes 10485784
  251.5 1.2 copy-done.7
  252.8 5.3 %shard_map.105 = (bf16[4,72,1024]{2,1,0:T(8,128)(2,1)S(1)}, bf16[4,72,1920]{2,1,0:T(8,128)(2,1)S(1)}) custom-call(s32[16,1,1024]{2,1,0:T(1,128)S(1)} %fusion.21.slot_ref, bf16[1024,1152]{1,0:T(8,128)(2,1)S(1)} %copy-done.4, bf16[16,512,640]{2,1,0:T(8,128)(2,1)S(1)} %copy-done.3, bf16[16,512,640]{2,1,0:T(8,128)(2,1)} %wu_ref.15, ...), custom_call_target="tpu_custom_call" | custom-call | flops 1170210816 | bytes 7864320 | tf_op jit(solution)/shard_map/pallas_call | solution.py:162
  262.7 8.6 %shard_map.106 = (f32[1024,512]{1,0:T(8,128)S(1)}, bf16[16,512,640]{2,1,0:T(8,128)(2,1)}, bf16[16,512,640]{2,1,0:T(8,128)(2,1)}, bf16[16,640,512]{2,1,0:T(8,128)(2,1)}) custom-call(s32[16,1,1024]{2,1,0:T(1,128)S(1)} %fusion.21.slot_ref, f32[16,1,1024]{2,1,0:T(1,128)S(1)} %compare_select_fusion.14.weight_ref, bf16[4,72,1024]{2,1,0:T(8,128)(2,1)S(1)} %copy-done.15, ...), custom_call_target="tpu_custom_call" | custom-call | flops 1245708288 | bytes 13107200 | tf_op jit(solution)/shard_map/pallas_call | solution.py:198
  271.3 8.7 %shard_map.107 = (f32[1024,512]{1,0:T(8,128)S(1)}, bf16[16,512,640]{2,1,0:T(8,128)(2,1)}, bf16[16,512,640]{2,1,0:T(8,128)(2,1)}, bf16[16,640,512]{2,1,0:T(8,128)(2,1)}) custom-call(s32[16,1,1024]{2,1,0:T(1,128)S(1)} %fusion.21.slot_ref, ...), custom_call_target="tpu_custom_call", output_to_operand_aliasing={{1}: (7, {}), {2}: (8, {}), {3}: (9, {})} | custom-call | flops 1245708288 | bytes 13107200 | tf_op jit(solution)/shard_map/pallas_call | solution.py:198
  280.0 8.6 %shard_map.108 = (f32[1024,512]{1,0:T(8,128)S(1)}, bf16[16,512,640]{2,1,0:T(8,128)(2,1)}, bf16[16,512,640]{2,1,0:T(8,128)(2,1)}, bf16[16,640,512]{2,1,0:T(8,128)(2,1)}) custom-call(s32[16,1,1024]{2,1,0:T(1,128)S(1)} %fusion.21.slot_ref, ...), custom_call_target="tpu_custom_call", output_to_operand_aliasing={{1}: (7, {}), {2}: (8, {}), {3}: (9, {})} | custom-call | flops 1245708288 | bytes 13107200 | tf_op jit(solution)/shard_map/pallas_call | solution.py:198
  288.6 25.0 %all-reduce.11.cloned.1.call-done.sum_ref = bf16[4,72,1920]{2,1,0:T(8,128)(2,1)} async-done(((bf16[4,72,1920]{2,1,0:T(8,128)(2,1)}), bf16[4,72,1920]{2,1,0:T(8,128)(2,1)}) %all-reduce.11.cloned.1.call-update) | async-done | bytes 1105936 | tf_op jit(solution)/shard_map/psum | solution.py:276
  313.6 1.2 copy-done.11
  314.9 8.5 %shard_map.109 = (f32[1024,512]{1,0:T(8,128)S(1)}, bf16[16,512,640]{2,1,0:T(8,128)(2,1)}, bf16[16,512,640]{2,1,0:T(8,128)(2,1)}, bf16[16,640,512]{2,1,0:T(8,128)(2,1)}) custom-call(s32[16,1,1024]{2,1,0:T(1,128)S(1)} %fusion.21.slot_ref, ...), custom_call_target="tpu_custom_call", output_to_operand_aliasing={{1}: (7, {}), {2}: (8, {}), {3}: (9, {})} | custom-call | flops 1245708288 | bytes 13107200 | tf_op jit(solution)/shard_map/pallas_call | solution.py:198
  324.5 32.5 %reduce-scatter.2.cloned.1.call-done = bf16[128,512]{1,0:T(8,128)(2,1)} async-done(((bf16[1024,512]{1,0:T(8,128)(2,1)}), bf16[128,512]{1,0:T(8,128)(2,1)}) %reduce-scatter.2.cloned.1.call-update) | async-done | bytes 131088 | tf_op jit(solution)/shard_map/reduce_scatter | solution.py:282
  (70 shorter events, 14.7 us)
Async XLA Ops:
  7.2 39.6 %all-gather.2.cloned.1.call-start = ((), (), s32[]{:S(2)}) async-start(), calls=%async_computation.1 | async-start | bytes 2654208 | tf_op jit(solution)/shard_map/all_gather | solution.py:254
  12.3 103.3 %all-reduce.5.cloned.1.call-start = ((), (), s32[]{:S(2)}) async-start(), calls=%async_computation.2 | async-start | bytes 2211840 | tf_op jit(solution)/shard_map/psum | solution.py:276
  12.4 49.7 %copy-start.24 = (f32[16]{0:T(128)}, f32[16]{0:T(128)S(1)}, u32[]{:S(2)}) copy-start(f32[16]{0:T(128)S(1)} %add_convert_fusion) | copy-start | bytes 196
  46.8 9.1 %copy-start = (bf16[16,512,640]{2,1,0:T(8,128)(2,1)S(1)}, bf16[16,512,640]{2,1,0:T(8,128)(2,1)}, u32[]{:S(2)}) copy-start(bf16[16,512,640]{2,1,0:T(8,128)(2,1)} %wg_ref.15) | copy-start | bytes 31457284
  46.8 9.1 %copy-start.4 = (bf16[1024,1152]{1,0:T(8,128)(2,1)S(1)}, bf16[1024,1152]{1,0:T(8,128)(2,1)}, u32[]{:S(2)}) copy-start(bf16[1024,1152]{1,0:T(8,128)(2,1)} %all-gather.2.cloned.1.call-done.tok_ref) | copy-start | bytes 7077892
  54.9 7.2 %copy-start.22 = (f32[1024]{0:T(1024)}, f32[1024]{0:T(1024)S(1)}, u32[]{:S(2)}) copy-start(f32[1024]{0:T(1024)S(1)} %get-tuple-element.72) | copy-start | bytes 12292
  62.9 118.5 %all-reduce.7.cloned.1.call-start = ((), (), s32[]{:S(2)}) async-start(), calls=%async_computation.3 | async-start | bytes 2211840 | tf_op jit(solution)/shard_map/psum | solution.py:276
  115.6 4.0 %copy-start.1 = (bf16[16,512,640]{2,1,0:T(8,128)(2,1)S(1)}, bf16[16,512,640]{2,1,0:T(8,128)(2,1)}, u32[]{:S(2)}) copy-start(bf16[16,512,640]{2,1,0:T(8,128)(2,1)} %wg_ref.15) | copy-start | bytes 31457284
  119.6 1.2 copy-start.9
  127.8 119.7 %all-reduce.9.cloned.1.call-start = ((), (), s32[]{:S(2)}) async-start(), calls=%async_computation.4 | async-start | bytes 2211840 | tf_op jit(solution)/shard_map/psum | solution.py:276
  181.5 4.0 %copy-start.2 = (bf16[16,512,640]{2,1,0:T(8,128)(2,1)S(1)}, bf16[16,512,640]{2,1,0:T(8,128)(2,1)}, u32[]{:S(2)}) copy-start(bf16[16,512,640]{2,1,0:T(8,128)(2,1)} %wg_ref.15) | copy-start | bytes 31457284
  185.4 1.2 copy-start.5
  193.9 67.7 %copy-start.10 = (bf16[4,72,1920]{2,1,0:T(8,128)(2,1)S(1)}, bf16[4,72,1920]{2,1,0:T(8,128)(2,1)}, u32[]{:S(2)}) copy-start(bf16[4,72,1920]{2,1,0:T(8,128)(2,1)} %all-reduce.5.cloned.1.call-done.rest_0_.sum_ref) | copy-start | bytes 3317764
  193.9 119.7 %all-reduce.11.cloned.1.call-start = ((), (), s32[]{:S(2)}) async-start(), calls=%async_computation.5 | async-start | bytes 2211840 | tf_op jit(solution)/shard_map/psum | solution.py:276
  247.5 4.0 %copy-start.3 = (bf16[16,512,640]{2,1,0:T(8,128)(2,1)S(1)}, bf16[16,512,640]{2,1,0:T(8,128)(2,1)}, u32[]{:S(2)}) copy-start(bf16[16,512,640]{2,1,0:T(8,128)(2,1)} %wg_ref.15) | copy-start | bytes 31457284
  251.5 1.2 copy-start.7
  260.0 97.1 %reduce-scatter.2.cloned.1.call-start = ((), (), s32[]{:S(2)}) async-start(), calls=%async_computation.6 | async-start | bytes 1179648 | tf_op jit(solution)/shard_map/reduce_scatter | solution.py:282
  261.6 1.1 copy-start.15
  262.7 8.6 %copy-start.6 = (bf16[4,72,1920]{2,1,0:T(8,128)(2,1)S(1)}, bf16[4,72,1920]{2,1,0:T(8,128)(2,1)}, u32[]{:S(2)}) copy-start(bf16[4,72,1920]{2,1,0:T(8,128)(2,1)} %all-reduce.7.cloned.1.call-done.rest_0_.sum_ref) | copy-start | bytes 3317764
  262.7 8.6 %copy-start.17 = (bf16[4,72,1024]{2,1,0:T(8,128)(2,1)S(1)}, bf16[4,72,1024]{2,1,0:T(8,128)(2,1)}, u32[]{:S(2)}) copy-start(bf16[4,72,1024]{2,1,0:T(8,128)(2,1)} %copy-done.16) | copy-start | bytes 1769476
  271.3 8.7 %copy-start.8 = (bf16[4,72,1920]{2,1,0:T(8,128)(2,1)S(1)}, bf16[4,72,1920]{2,1,0:T(8,128)(2,1)}, u32[]{:S(2)}) copy-start(bf16[4,72,1920]{2,1,0:T(8,128)(2,1)} %all-reduce.9.cloned.1.call-done.rest_0_.sum_ref) | copy-start | bytes 3317764
  271.3 8.7 %copy-start.21 = (bf16[4,72,1024]{2,1,0:T(8,128)(2,1)S(1)}, bf16[4,72,1024]{2,1,0:T(8,128)(2,1)}, u32[]{:S(2)}) copy-start(bf16[4,72,1024]{2,1,0:T(8,128)(2,1)} %copy-done.20) | copy-start | bytes 1769476
  280.0 33.6 %copy-start.19 = (bf16[4,72,1024]{2,1,0:T(8,128)(2,1)S(1)}, bf16[4,72,1024]{2,1,0:T(8,128)(2,1)}, u32[]{:S(2)}) copy-start(bf16[4,72,1024]{2,1,0:T(8,128)(2,1)} %copy-done.18) | copy-start | bytes 1769476
  313.6 1.2 copy-start.11
  (7 other events, 5.9 us)
Sparse Core Ops, SparseCore 0:
  12.4 34.3 all-gather.1
  63.1 52.4 all-reduce.4
  127.9 53.4 all-reduce.6
  194.0 53.4 all-reduce.8
  260.1 53.4 all-reduce.10
  324.7 32.3 reduce-scatter.1

commit v2 on v1

--- a/solution.py
+++ b/solution.py
@@ -94,8 +94,7 @@
     return rows == slot_row
 
 
-def pre_kernel(slot_ref, tok_ref, wg_ref, wu_ref, wd_ref, *rest):
-    rows_ref, part_ref = rest[-2:]
+def pre_kernel(slot_ref, tok_ref, wg_ref, wu_ref, wd_ref, rows_ref, part_ref):
     slot_rows = rows_ref.shape[1]
     half = wg_ref.shape[1]
     ffw = wg_ref.shape[2]
@@ -112,14 +111,9 @@
     part_ref[0, :, 2 * ffw :] = back.astype(jnp.bfloat16)
 
 
-def post_kernel(slot_ref, weight_ref, rows_ref, sum_ref, wg_ref, wu_ref, *rest):
-    acc_in, total_ref, gg_ref, gu_ref, gd_ref = rest[0], *rest[-4:]
-    slot_rows = rows_ref.shape[1]
-    half = wg_ref.shape[1]
-    ffw = wg_ref.shape[2]
+def deltas(slot_ref, weight_ref, sum_ref, slot_rows, ffw):
     hit = routes(slot_ref[0], slot_rows)
     weight = jnp.sum(jnp.where(hit, weight_ref[0], 0.0), axis=1, keepdims=True)
-    place = hit.astype(jnp.bfloat16)
     pre_gate = sum_ref[0, :, :ffw].astype(jnp.float32)
     pre_up = sum_ref[0, :, ffw : 2 * ffw].astype(jnp.float32)
     pre_back = sum_ref[0, :, 2 * ffw :].astype(jnp.float32)
@@ -129,35 +123,52 @@
     hidden = (silu * pre_up).astype(jnp.bfloat16)
     gate_delta = (d_hidden * pre_up * sig * (1.0 + pre_gate * (1.0 - sig))).astype(jnp.bfloat16)
     up_delta = (d_hidden * silu).astype(jnp.bfloat16)
+    return hit, weight, hidden, gate_delta, up_delta
+
+
+NT = (((1,), (1,)), ((), ()))
+TN = (((0,), (0,)), ((), ()))
+
+
+def back_kernel(slot_ref, weight_ref, sum_ref, wg_ref, wu_ref, out_ref, total_ref):
+    ffw = wg_ref.shape[2]
+    hit, _, _, gate_delta, up_delta = deltas(slot_ref, weight_ref, sum_ref, sum_ref.shape[1], ffw)
+    f32 = jnp.float32
+    back = lax.dot_general(gate_delta, wg_ref[0], NT, preferred_element_type=f32)
+    back = back + lax.dot_general(up_delta, wu_ref[0], NT, preferred_element_type=f32)
+    place = hit.astype(jnp.bfloat16)
+    mine = lax.dot_general(place, back.astype(jnp.bfloat16), TN, preferred_element_type=f32)
+
+    @pl.when(pl.program_id(0) == 0)
+    def _():
+        total_ref[...] = mine
+
+    @pl.when(pl.program_id(0) > 0)
+    def _():
+        total_ref[...] += mine
+
+    @pl.when(pl.program_id(0) == pl.num_programs(0) - 1)
+    def _():
+        out_ref[...] = total_ref[...].astype(jnp.bfloat16)
+
+
+def grad_kernel(slot_ref, weight_ref, rows_ref, sum_ref, gg_ref, gu_ref, gd_ref):
+    half, ffw = gg_ref.shape[1:]
+    _, weight, hidden, gate_delta, up_delta = deltas(
+        slot_ref, weight_ref, sum_ref, rows_ref.shape[1], ffw
+    )
     rows_in = rows_ref[0, :, :half]
     scaled = (weight * rows_ref[0, :, half:].astype(jnp.float32)).astype(jnp.bfloat16)
-    nt = (((1,), (1,)), ((), ()))
-    tn = (((0,), (0,)), ((), ()))
-    f32 = jnp.float32
-    back = lax.dot_general(gate_delta, wg_ref[0], nt, preferred_element_type=f32)
-    back = back + lax.dot_general(up_delta, wu_ref[0], nt, preferred_element_type=f32)
-    gg_ref[0] = lax.dot_general(rows_in, gate_delta, tn, preferred_element_type=f32).astype(
-        jnp.bfloat16
-    )
-    gu_ref[0] = lax.dot_general(rows_in, up_delta, tn, preferred_element_type=f32).astype(
-        jnp.bfloat16
-    )
-    gd_ref[0] = lax.dot_general(hidden, scaled, tn, preferred_element_type=f32).astype(jnp.bfloat16)
-
-    @pl.when(pl.program_id(0) == 0)
-    def _():
-        total_ref[...] = acc_in[...]
-
-    total_ref[...] += lax.dot_general(
-        place, back.astype(jnp.bfloat16), tn, preferred_element_type=f32
-    )
-
-
-def pre_call(first, count, slot, gathered, w_gate, w_up, w_down, slot_rows, after):
-    quarter, ffw = w_gate.shape[1:]
+    f32, b16 = jnp.float32, jnp.bfloat16
+    gg_ref[0] = lax.dot_general(rows_in, gate_delta, TN, preferred_element_type=f32).astype(b16)
+    gu_ref[0] = lax.dot_general(rows_in, up_delta, TN, preferred_element_type=f32).astype(b16)
+    gd_ref[0] = lax.dot_general(hidden, scaled, TN, preferred_element_type=f32).astype(b16)
+
+
+def pre_call(slot, gathered, w_gate, w_up, w_down, slot_rows):
+    count, quarter, ffw = w_gate.shape
     token_count = slot.shape[2]
-    mine = lambda i: (first + i, 0, 0)
-    local = lambda i: (i, 0, 0)
+    mine = lambda i: (i, 0, 0)
     flops = 2 * count * slot_rows * quarter * (2 * token_count + 3 * ffw)
     return pl.pallas_call(
         pre_kernel,
@@ -168,11 +179,10 @@
             pl.BlockSpec((1, quarter, ffw), mine),
             pl.BlockSpec((1, quarter, ffw), mine),
             pl.BlockSpec((1, ffw, quarter), mine),
-        ]
-        + [pl.BlockSpec(memory_space=pl.ANY)] * len(after),
+        ],
         out_specs=[
-            pl.BlockSpec((1, slot_rows, 2 * quarter), local),
-            pl.BlockSpec((1, slot_rows, 3 * ffw), local),
+            pl.BlockSpec((1, slot_rows, 2 * quarter), mine),
+            pl.BlockSpec((1, slot_rows, 3 * ffw), mine),
         ],
         out_shape=[
             jax.ShapeDtypeStruct((count, slot_rows, 2 * quarter), jnp.bfloat16),
@@ -182,56 +192,64 @@
         cost_estimate=pl.CostEstimate(
             flops=flops, bytes_accessed=count * 6 * quarter * ffw, transcendentals=0
         ),
-    )(slot, gathered, w_gate, w_up, w_down, *after)
-
-
-def post_call(first, count, slot, weight, rows, summed, w_gate, w_up, total, grads):
-    quarter, ffw = w_gate.shape[1:]
-    local_count = w_gate.shape[0]
+    )(slot, gathered, w_gate, w_up, w_down)
+
+
+def back_call(slot, weight, summed, w_gate, w_up):
+    local_count, quarter, ffw = w_gate.shape
     token_count = slot.shape[2]
+    slot_rows = summed.shape[1]
+    mine = lambda i: (i, 0, 0)
+    return pl.pallas_call(
+        back_kernel,
+        grid=(local_count,),
+        in_specs=[
+            pl.BlockSpec((1, 1, token_count), mine),
+            pl.BlockSpec((1, 1, token_count), mine),
+            pl.BlockSpec((1, slot_rows, 3 * ffw), mine),
+            pl.BlockSpec((1, quarter, ffw), mine),
+            pl.BlockSpec((1, quarter, ffw), mine),
+        ],
+        out_specs=pl.BlockSpec((token_count, quarter), lambda i: (0, 0)),
+        out_shape=jax.ShapeDtypeStruct((token_count, quarter), jnp.bfloat16),
+        scratch_shapes=[pltpu.VMEM((token_count, quarter), jnp.float32)],
+        compiler_params=pltpu.CompilerParams(vmem_limit_bytes=32 << 20),
+        cost_estimate=pl.CostEstimate(
+            flops=2 * local_count * slot_rows * quarter * (2 * ffw + token_count),
+            bytes_accessed=local_count * 4 * quarter * ffw,
+            transcendentals=0,
+        ),
+    )(slot, weight, summed, w_gate, w_up)
+
+
+def grad_call(slot, weight, rows, summed, quarter, ffw):
+    local_count, _, token_count = slot.shape
     slot_rows = rows.shape[1]
-    mine = lambda i: (first + i, 0, 0)
-    local = lambda i: (i, 0, 0)
-    whole = lambda i: (0, 0)
+    mine = lambda i: (i, 0, 0)
     up_shape = jax.ShapeDtypeStruct((local_count, quarter, ffw), jnp.bfloat16)
     down_shape = jax.ShapeDtypeStruct((local_count, ffw, quarter), jnp.bfloat16)
     return pl.pallas_call(
-        post_kernel,
-        grid=(count,),
+        grad_kernel,
+        grid=(local_count,),
         in_specs=[
             pl.BlockSpec((1, 1, token_count), mine),
             pl.BlockSpec((1, 1, token_count), mine),
-            pl.BlockSpec((1, slot_rows, 2 * quarter), local),
-            pl.BlockSpec((1, slot_rows, 3 * ffw), local),
-            pl.BlockSpec((1, quarter, ffw), mine),
-            pl.BlockSpec((1, quarter, ffw), mine),
-            pl.BlockSpec((token_count, quarter), whole),
-        ]
-        + [pl.BlockSpec(memory_space=pl.ANY)] * len(grads),
+            pl.BlockSpec((1, slot_rows, 2 * quarter), mine),
+            pl.BlockSpec((1, slot_rows, 3 * ffw), mine),
+        ],
         out_specs=[
-            pl.BlockSpec((token_count, quarter), whole),
             pl.BlockSpec((1, quarter, ffw), mine),
             pl.BlockSpec((1, quarter, ffw), mine),
             pl.BlockSpec((1, ffw, quarter), mine),
         ],
-        out_shape=[
-            jax.ShapeDtypeStruct((token_count, quarter), jnp.float32),
-            up_shape,
-            up_shape,
-            down_shape,
-        ],
-        input_output_aliases={7 + i: 1 + i for i in range(len(grads))},
-        compiler_params=pltpu.CompilerParams(vmem_limit_bytes=40 << 20),
+        out_shape=[up_shape, up_shape, down_shape],
+        compiler_params=pltpu.CompilerParams(vmem_limit_bytes=32 << 20),
         cost_estimate=pl.CostEstimate(
-            flops=2 * count * slot_rows * quarter * (5 * ffw + token_count),
-            bytes_accessed=count * 10 * quarter * ffw,
+            flops=6 * local_count * slot_rows * quarter * ffw,
+            bytes_accessed=local_count * 6 * quarter * ffw,
             transcendentals=0,
         ),
-    )(slot, weight, rows, summed, w_gate, w_up, total, *grads)
-
-
-CHUNKS = 4
-LAG = 1
+    )(slot, weight, rows, summed)
 
 
 def gathered_body(tokens, out_grad, expert_ids, route_weight, w_gate, w_up, w_down):
@@ -265,24 +283,11 @@
         weight = jnp.where(here, facts[2 * picks + k][None, :], weight)
     slot = slot.astype(jnp.int32)[:, None, :]
     weight = weight[:, None, :]
-    count = local_count // CHUNKS
-    summed, routed = [], []
-    for c in range(CHUNKS):
-        after = summed[c - LAG : c - LAG + 1] if c >= LAG else []
-        got, part = pre_call(
-            c * count, count, slot, everyone, w_gate, w_up, w_down, slot_rows, after
-        )
-        routed.append(got)
-        summed.append(lax.psum(part, "rep"))
-    total, grads = jnp.zeros((token_count, quarter), jnp.float32), []
-    for c in range(CHUNKS):
-        total, *grads = post_call(
-            c * count, count, slot, weight, routed[c], summed[c], w_gate, w_up, total, grads
-        )
-    token_grad = lax.psum_scatter(
-        total.astype(jnp.bfloat16), "ep", scatter_dimension=0, tiled=True
-    )
-    return (token_grad, *grads)
+    routed, part = pre_call(slot, everyone, w_gate, w_up, w_down, slot_rows)
+    summed = lax.psum(part, "rep")
+    total = back_call(slot, weight, summed, w_gate, w_up)
+    token_grad = lax.psum_scatter(total, "ep", scatter_dimension=0, tiled=True)
+    return (token_grad, *grad_call(slot, weight, routed, summed, quarter, ffw))
 
 
 def solution(mesh):

time: 365 us -> 250 us (0.68)
  waiting for transfers between devices: 252 us -> 156 us
  local copies, waits for them, and re-layouts: 27.6 us -> 14.1 us
    psum x4 -> x1, waiting for transfers between devices: 185 us -> 107 us  [gathered_body(): summed = lax.psum(part, 'rep')]
    reduce_scatter x1, waiting for transfers between devices: 32.5 us -> 15.1 us  [gathered_body(): token_grad = lax.psum_scatter(total, 'ep', scatter_dimension=0, tiled=True)]
    unnamed x52 -> x14, local copies, waits for them, and re-layouts: 25.5 us -> 12.2 us
    pallas_call x4 -> x1, Pallas kernels: 23.1 us -> 18.7 us  [pre_call(): pl.pallas_call(pre_kernel, grid=(count,), in_specs=[pl.BlockSpec((1, 1, t...]
    pallas_call x4 -> x2, Pallas kernels: 34.4 us -> 36.8 us  [the longest x1 21.2 us: back_call(): pl.pallas_call(back_kernel, grid=(local_count,), in_specs=[pl.BlockSpec((...]
  transfers between devices with their start and end apart: 6 -> 3, of which waited for: 6 -> 3; matrix products, arithmetic and copies ran while one was open for 0% -> 0% of each run, Pallas kernels for 7% -> 6%
where the time goes in v2:
time: 250 us
  waiting for transfers between devices  156 us (62%)
  Pallas kernels  55.5 us (22%)
  local copies, waits for them, and re-layouts  14.1 us (6%)
  between operations  13.8 us (6%)
  other arithmetic  9.72 us (4%)
    psum x1, waiting for transfers between devices, gathered_body(): summed = lax.psum(part, 'rep')  107 us
    all_gather x1, waiting for transfers between devices, gathered_body(): everyone = lax.all_gather(packed, 'ep', axis=0, tiled=True)  34.4 us
    pallas_call x1, Pallas kernels, back_call(): pl.pallas_call(back_kernel, grid=(local_count,), in_specs=[pl.BlockSpec((...  21.2 us
    pallas_call x1, Pallas kernels, pre_call(): pl.pallas_call(pre_kernel, grid=(count,), in_specs=[pl.BlockSpec((1, 1, t...  18.7 us
    pallas_call x1, Pallas kernels, grad_call(): pl.pallas_call(grad_kernel, grid=(local_count,), in_specs=[pl.BlockSpec((...  15.6 us
    reduce_scatter x1, waiting for transfers between devices, gathered_body(): token_grad = lax.psum_scatter(total, 'ep', scatter_dimension=0, tiled=True)  15.1 us
    unnamed x14, local copies, waits for them, and re-layouts  12.2 us
    slice x1, other arithmetic, gathered_body(): weight = jnp.where(here, facts[2 * picks + k][None, :], weight)  5.09 us
  transfers between devices with their start and end apart: 3, of which 3 were waited for; matrix products, arithmetic and copies ran while one was open for 0% of the time, Pallas kernels for 6%

profile of v2, /device:TPU:0, one launch (start us, length us, event | category | flops | bytes accessed | tf_op | source)
XLA Modules:
  0.0 249.7 jit_solution(9194386514724208616)
XLA Ops:
  7.2 0.8 copy.17
  8.0 0.7 convert_element_type.61
  8.7 0.2 convert_reduce_fusion
  8.9 0.2 fusion.23
  9.1 0.4 select_reduce_fusion
  9.5 0.1 copy.18
  9.7 0.8 copy.19
  10.5 1.8 concatenate.3
  12.4 34.4 %all-gather.2.cloned.1.call-done.tok_ref = bf16[1024,1152]{1,0:T(8,128)(2,1)} async-done(((bf16[128,1152]{1,0:T(8,128)(2,1)}), bf16[1024,1152]{1,0:T(8,128)(2,1)}) %all-gather.2.cloned.1.call-update) | async-done | bytes 2359312 | tf_op jit(solution)/shard_map/all_gather | solution.py:272
  46.8 1.1 convert_bitcast_fusion
  47.9 5.1 %slice_reduce_fusion.7 = (f32[1024]{0:T(1024)S(1)}, f32[1024]{0:T(1024)S(1)}, f32[1024]{0:T(1024)S(1)}, f32[1024]{0:T(1024)S(1)}, f32[1024]{0:T(1024)S(1)}, /*in...) fusion(f32[24,1024]{0,1:T(8,128)S(1)} %convert_bitcast_fusion), kind=kLoop, calls=%fused_computation.31 | loop fusion | flops 16384 | bytes 155648 | tf_op jit(solution)/shard_map/slice | solution.py:283
  53.0 1.4 slice_reduce_fusion.15
  54.5 0.4 fusion.21.slot_ref
  54.9 18.7 %shard_map.102 = (bf16[16,72,1024]{2,1,0:T(8,128)(2,1)S(1)}, bf16[16,72,1920]{2,1,0:T(8,128)(2,1)S(1)}) custom-call(s32[16,1,1024]{2,1,0:T(1,128)S(1)} %fusion.21.slot_ref, bf16[1024,1152]{1,0:T(8,128)(2,1)S(1)} %copy-done.5, bf16[16,512,640]{2,1,0:T(8,128)(2,1)S(1)} %copy-done, bf16[16,512,640]{2,1,0:T(8,128)(2,1)} %wu_ref.3, bf16[16,640,512]{2,1,0:T(8,128)(2,1)} %wd_ref.1), custom_call_target="tpu_custom_call" | custom-call | flops 4680843264 | bytes 31457280 | tf_op jit(solution)/shard_map/pallas_call | solution.py:173
  73.6 2.1 copy-done.4
  75.7 0.0 reduce-scatter.2.cloned.1.call-start
  75.8 0.3 compare_select_fusion.14.weight_ref
  76.1 106.6 %all-reduce.2.cloned.1.call-done.sum_ref = bf16[16,72,1920]{2,1,0:T(8,128)(2,1)} async-done(((bf16[16,72,1920]{2,1,0:T(8,128)(2,1)}), bf16[16,72,1920]{2,1,0:T(8,128)(2,1)}) %all-reduce.2.cloned.1.call-update) | async-done | bytes 4423696 | tf_op jit(solution)/shard_map/psum | solution.py:287
  182.7 4.0 %copy-done.1 = bf16[16,512,640]{2,1,0:T(8,128)(2,1)S(1)} copy-done((bf16[16,512,640]{2,1,0:T(8,128)(2,1)S(1)}, bf16[16,512,640]{2,1,0:T(8,128)(2,1)}, u32[]{:S(2)}) %copy-start.1) | copy-done | bytes 10485784
  186.7 2.3 copy-done.2
  189.0 21.2 %shard_map.103 = bf16[1024,512]{1,0:T(8,128)(2,1)} custom-call(s32[16,1,1024]{2,1,0:T(1,128)S(1)} %fusion.21.slot_ref, f32[16,1,1024]{2,1,0:T(1,128)S(1)} %compare_select_fusion.14.weight_ref, bf16[16,72,1920]{2,1,0:T(8,128)(2,1)S(1)} %copy-done.2, bf16[16,512,640]{2,1,0:T(8,128)(2,1)S(1)} %copy-done.1, bf16[16,512,640]{2,1,0:T(8,128)(2,1)} %wu_ref.3), custom_call_target="tpu_custom_call" | custom-call | flops 2717908992 | bytes 20971520 | tf_op jit(solution)/shard_map/pallas_call | solution.py:203
  210.2 2.2 copy-done.3
  212.5 15.6 %shard_map.104 = (bf16[16,512,640]{2,1,0:T(8,128)(2,1)}, bf16[16,512,640]{2,1,0:T(8,128)(2,1)}, bf16[16,640,512]{2,1,0:T(8,128)(2,1)}) custom-call(s32[16,1,1024]{2,1,0:T(1,128)S(1)} %fusion.21.slot_ref, f32[16,1,1024]{2,1,0:T(1,128)S(1)} %compare_select_fusion.14.weight_ref, bf16[16,72,1024]{2,1,0:T(8,128)(2,1)S(1)} %get-tuple-element.10.rows_ref, ...), custom_call_target="tpu_custom_call" | custom-call | flops 2264924160 | bytes 31457280 | tf_op jit(solution)/shard_map/pallas_call | solution.py:231
  228.1 15.1 %reduce-scatter.2.cloned.1.call-done = bf16[128,512]{1,0:T(8,128)(2,1)} async-done(((bf16[1024,512]{1,0:T(8,128)(2,1)}), bf16[128,512]{1,0:T(8,128)(2,1)}) %reduce-scatter.2.cloned.1.call-update) | async-done | bytes 131088 | tf_op jit(solution)/shard_map/reduce_scatter | solution.py:289
  (16 shorter events, 0.2 us)
Async XLA Ops:
  7.2 39.6 %all-gather.2.cloned.1.call-start = ((), (), s32[]{:S(2)}) async-start(), calls=%async_computation.1 | async-start | bytes 2654208 | tf_op jit(solution)/shard_map/all_gather | solution.py:272
  12.3 170.4 %all-reduce.2.cloned.1.call-start = ((), (), s32[]{:S(2)}) async-start(), calls=%async_computation.2 | async-start | bytes 8847360 | tf_op jit(solution)/shard_map/psum | solution.py:287
  46.8 8.1 %copy-start = (bf16[16,512,640]{2,1,0:T(8,128)(2,1)S(1)}, bf16[16,512,640]{2,1,0:T(8,128)(2,1)}, u32[]{:S(2)}) copy-start(bf16[16,512,640]{2,1,0:T(8,128)(2,1)} %wg_ref.3) | copy-start | bytes 31457284
  46.8 8.1 %copy-start.5 = (bf16[1024,1152]{1,0:T(8,128)(2,1)S(1)}, bf16[1024,1152]{1,0:T(8,128)(2,1)}, u32[]{:S(2)}) copy-start(bf16[1024,1152]{1,0:T(8,128)(2,1)} %all-gather.2.cloned.1.call-done.tok_ref) | copy-start | bytes 7077892
  73.6 2.1 copy-start.4
  75.7 167.4 %reduce-scatter.2.cloned.1.call-start = ((), (), s32[]{:S(2)}) async-start(), calls=%async_computation.3 | async-start | bytes 1179648 | tf_op jit(solution)/shard_map/reduce_scatter | solution.py:289
  182.7 4.0 %copy-start.1 = (bf16[16,512,640]{2,1,0:T(8,128)(2,1)S(1)}, bf16[16,512,640]{2,1,0:T(8,128)(2,1)}, u32[]{:S(2)}) copy-start(bf16[16,512,640]{2,1,0:T(8,128)(2,1)} %wg_ref.3) | copy-start | bytes 31457284
  186.7 2.3 copy-start.2
  210.2 2.3 copy-start.3
Sparse Core Ops, SparseCore 0:
  12.4 34.3 all-gather.1
  75.8 106.8 all-reduce.1
  210.3 32.7 reduce-scatter.1

commit v3 on v2

--- a/solution.py
+++ b/solution.py
@@ -252,6 +252,45 @@
     )(slot, weight, rows, summed)
 
 
+def swap(value, bit):
+    return lax.ppermute(value, "rep", [(r, r ^ bit) for r in range(lax.axis_size("rep"))])
+
+
+def halves(value, side):
+    pair = value.reshape((2, value.shape[0] // 2) + value.shape[1:])
+    return (
+        lax.dynamic_index_in_dim(pair, side, 0, keepdims=False),
+        lax.dynamic_index_in_dim(pair, 1 - side, 0, keepdims=False),
+    )
+
+
+def added(kept, came):
+    return (kept.astype(jnp.float32) + came.astype(jnp.float32)).astype(jnp.bfloat16)
+
+
+def joined(kept, came, side):
+    low = jnp.where(side == 0, kept, came)
+    return jnp.concatenate([low, jnp.where(side == 0, came, kept)], axis=0)
+
+
+def rep_sum(part):
+    rank = lax.axis_index("rep")
+    sides = {1: rank % 2, 2: rank // 2}
+    count = part.shape[0] // 2
+    paths = [(part[:count], (1, 2)), (part[count:], (2, 1))]
+    values = [value for value, _ in paths]
+    for step in (0, 1):
+        split = [halves(v, sides[order[step]]) for v, (_, order) in zip(values, paths)]
+        came = [swap(other, order[step]) for (_, other), (_, order) in zip(split, paths)]
+        values = [added(kept, new) for (kept, _), new in zip(split, came)]
+    for step in (1, 0):
+        came = [swap(v, order[step]) for v, (_, order) in zip(values, paths)]
+        values = [
+            joined(v, new, sides[order[step]]) for v, new, (_, order) in zip(values, came, paths)
+        ]
+    return jnp.concatenate(values, axis=0)
+
+
 def gathered_body(tokens, out_grad, expert_ids, route_weight, w_gate, w_up, w_down):
     ep_ranks = lax.axis_size("ep")
     local_count, quarter, ffw = w_gate.shape
@@ -284,7 +323,7 @@
     slot = slot.astype(jnp.int32)[:, None, :]
     weight = weight[:, None, :]
     routed, part = pre_call(slot, everyone, w_gate, w_up, w_down, slot_rows)
-    summed = lax.psum(part, "rep")
+    summed = rep_sum(part)
     total = back_call(slot, weight, summed, w_gate, w_up)
     token_grad = lax.psum_scatter(total, "ep", scatter_dimension=0, tiled=True)
     return (token_grad, *grad_call(slot, weight, routed, summed, quarter, ffw))
@@ -301,7 +340,7 @@
         P("ep", None, "rep"),
     )
     return jax.shard_map(
-        gathered_body if mesh.shape["ep"] <= 8 else body,
+        gathered_body if mesh.shape["ep"] <= 8 and mesh.shape["rep"] == 4 else body,
         mesh=mesh,
         in_specs=placed,
         out_specs=(

time: 250 us -> 227 us (0.908)
  waiting for transfers between devices: 156 us -> 108 us
  starting transfers between devices: 0.12 us -> 12.1 us
  other arithmetic: 9.72 us -> 20.8 us
    psum x1 -> x0, waiting for transfers between devices: 107 us -> none  [gathered_body(): summed = lax.psum(part, 'rep')]
    ppermute x0 -> x8, waiting for transfers between devices: none -> 61.1 us  [swap(): lax.ppermute(value, 'rep', [(r, r ^ bit) for r in range(lax.axis_size('re...]
    ppermute x0 -> x8, starting transfers between devices: none -> 12 us  [swap(): lax.ppermute(value, 'rep', [(r, r ^ bit) for r in range(lax.axis_size('re...]
    convert_element_type x0 -> x4, other arithmetic: none -> 5.62 us  [added(): (kept.astype(jnp.float32) + came.astype(jnp.float32)).astype(jnp.bfloat16)]
    unnamed x14 -> x48, local copies, waits for them, and re-layouts: 12.2 us -> 7.86 us
    squeeze x0 -> x4, local copies, waits for them, and re-layouts: none -> 3.29 us  [halves(): lax.dynamic_index_in_dim(pair, 1 - side, 0, keepdims=False)]
    concatenate x0 -> x3, other arithmetic: none -> 3.09 us  [the longest x1 2.86 us: rep_sum(): return jnp.concatenate(values, axis=0)]
  transfers between devices with their start and end apart: 3 -> 10, of which waited for: 3 -> 9; matrix products, arithmetic and copies ran while one was open for 0% -> 5% of each run, Pallas kernels for 6% -> 7%
where the time goes in v3:
time: 227 us; the launch traced here: 226 us
  waiting for transfers between devices  108 us (48%)
  Pallas kernels  55.8 us (25%)
  other arithmetic  20.8 us (9%)
  local copies, waits for them, and re-layouts  14.7 us (6%)
  between operations  14.4 us (6%)
  starting transfers between devices  12.1 us (5%)
    ppermute x8, waiting for transfers between devices, swap(): lax.ppermute(value, 'rep', [(r, r ^ bit) for r in range(lax.axis_size('re...  61.1 us
    all_gather x1, waiting for transfers between devices, gathered_body(): everyone = lax.all_gather(packed, 'ep', axis=0, tiled=True)  34.4 us
    pallas_call x1, Pallas kernels, back_call(): pl.pallas_call(back_kernel, grid=(local_count,), in_specs=[pl.BlockSpec((...  21.2 us
    pallas_call x1, Pallas kernels, pre_call(): pl.pallas_call(pre_kernel, grid=(count,), in_specs=[pl.BlockSpec((1, 1, t...  18.9 us
    pallas_call x1, Pallas kernels, grad_call(): pl.pallas_call(grad_kernel, grid=(local_count,), in_specs=[pl.BlockSpec((...  15.6 us
    reduce_scatter x1, waiting for transfers between devices, gathered_body(): token_grad = lax.psum_scatter(total, 'ep', scatter_dimension=0, tiled=True)  12.9 us
    ppermute x8, starting transfers between devices, swap(): lax.ppermute(value, 'rep', [(r, r ^ bit) for r in range(lax.axis_size('re...  12 us
    unnamed x48, local copies, waits for them, and re-layouts  7.86 us
  transfers between devices with their start and end apart: 10, of which 9 were waited for; matrix products, arithmetic and copies ran while one was open for 5% of the time, Pallas kernels for 7%

profile of v3, /device:TPU:0, one launch (start us, length us, event | category | flops | bytes accessed | tf_op | source)
XLA Modules:
  0.0 226.4 jit_solution(15913063483729174924)
XLA Ops:
  10.5 1.8 concatenate.12
  12.4 34.4 %all-gather.2.cloned.1.call-done.tok_ref = bf16[1024,1152]{1,0:T(8,128)(2,1)} async-done(((bf16[128,1152]{1,0:T(8,128)(2,1)}), bf16[1024,1152]{1,0:T(8,128)(2,1)}) %all-gather.2.cloned.1.call-update) | async-done | bytes 2359312 | tf_op jit(solution)/shard_map/all_gather | solution.py:311
  47.9 5.6 %slice_reduce_fusion.7 = (f32[1024]{0:T(1024)}, f32[1024]{0:T(1024)}, f32[1024]{0:T(1024)}, f32[1024]{0:T(1024)}, f32[1024]{0:T(1024)}, /*index=5*/f32[1024]{0:T...) fusion(f32[24,1024]{0,1:T(8,128)S(1)} %convert_bitcast_fusion), kind=kLoop, calls=%fused_computation.54 | loop fusion | flops 16384 | bytes 155648 | tf_op jit(solution)/shard_map/slice | solution.py:322
  55.9 18.9 %shard_map.102 = (bf16[16,72,1024]{2,1,0:T(8,128)(2,1)S(1)}, bf16[16,72,1920]{2,1,0:T(8,128)(2,1)S(1)}) custom-call(s32[16,1,1024]{2,1,0:T(1,128)S(1)} %fusion.25.slot_ref, bf16[1024,1152]{1,0:T(8,128)(2,1)S(1)} %copy-done.3, bf16[16,512,640]{2,1,0:T(8,128)(2,1)S(1)} %copy-done, bf16[16,512,640]{2,1,0:T(8,128)(2,1)} %wu_ref.3, bf16[16,640,512]{2,1,0:T(8,128)(2,1)} %wd_ref.1), custom_call_target="tpu_custom_call" | custom-call | flops 4680843264 | bytes 31457280 | tf_op jit(solution)/shard_map/pallas_call | solution.py:173
  74.9 1.7 fusion.35
  79.4 2.3 %dynamic-slice_bitcast_fusion = bf16[4,72,1920]{2,1,0:T(8,128)(2,1)} fusion(bf16[2,4,72,1920]{3,2,1,0:T(8,128)(2,1)} %bitcast.29, s32[]{:T(128)S(6)} %select_n.301), kind=kLoop, calls=%fused_computation.11 | loop fusion | bytes 2211844 | tf_op jit(solution)/shard_map/jit(dynamic_index_in_dim)/squeeze | solution.py:263
  83.1 21.4 %collective-permute-done = bf16[4,72,1920]{2,1,0:T(8,128)(2,1)} collective-permute-done((bf16[4,72,1920]{2,1,0:T(8,128)(2,1)S(1)}, bf16[4,72,1920]{2,1,0:T(8,128)(2,1)}, u32[]{:S(2)}, u32[]{:S(2)}) %collective-permute-start) | collective-permute-done | bytes 1105952 | tf_op jit(solution)/shard_map/ppermute | solution.py:256
  104.5 2.0 fusion.1
  106.6 1.5 collective-permute-start.1
  108.2 1.5 fusion
  112.0 8.5 %collective-permute-done.1 = bf16[2,72,1920]{2,1,0:T(8,128)(2,1)S(1)} collective-permute-done((bf16[2,72,1920]{2,1,0:T(8,128)(2,1)S(1)}, bf16[2,72,1920]{2,1,0:T(8,128)(2,1)S(1)}, u32[]{:S(2)}, u32[]{:S(2)}) %collective-permute-start.1) | collective-permute-done | bytes 552992 | tf_op jit(solution)/shard_map/ppermute | solution.py:256
  121.4 1.5 collective-permute-start.2
  122.9 1.6 collective-permute-done.5
  127.1 7.7 %collective-permute-done.2 = bf16[2,72,1920]{2,1,0:T(8,128)(2,1)} collective-permute-done((bf16[2,72,1920]{2,1,0:T(8,128)(2,1)}, bf16[2,72,1920]{2,1,0:T(8,128)(2,1)}, u32[]{:S(2)}, u32[]{:S(2)}) %collective-permute-start.2) | collective-permute-done | bytes 552992 | tf_op jit(solution)/shard_map/ppermute | solution.py:256
  136.2 1.5 collective-permute-start.3
  137.8 2.3 %collective-permute-done.6 = bf16[2,72,1920]{2,1,0:T(8,128)(2,1)S(1)} collective-permute-done((bf16[2,72,1920]{2,1,0:T(8,128)(2,1)S(1)}, bf16[2,72,1920]{2,1,0:T(8,128)(2,1)S(1)}, u32[]{:S(2)}, u32[]{:S(2)}) %collective-permute-start.6) | collective-permute-done | bytes 552992 | tf_op jit(solution)/shard_map/ppermute | solution.py:256
  140.4 1.6 collective-permute-start.7
  142.5 19.6 %collective-permute-done.3 = bf16[4,72,1920]{2,1,0:T(8,128)(2,1)S(1)} collective-permute-done((bf16[4,72,1920]{2,1,0:T(8,128)(2,1)S(1)}, bf16[4,72,1920]{2,1,0:T(8,128)(2,1)S(1)}, u32[]{:S(2)}, u32[]{:S(2)}) %collective-permute-start.3) | collective-permute-done | bytes 1105952 | tf_op jit(solution)/shard_map/ppermute | solution.py:256
  162.6 2.9 %pad_maximum_fusion.sum_ref = bf16[16,72,1920]{2,1,0:T(8,128)(2,1)S(1)} fusion(bf16[4,72,1920]{2,1,0:T(8,128)(2,1)S(1)} %get-tuple-element.43, bf16[4,72,1920]{2,1,0:T(8,128)(2,1)S(1)} %get-tuple-element.42, bf16[4,72,1920]{2,1,0:T(8,128)(2,1)S(1)} %get-tuple-element.41, bf16[4,72,1920]{2,1,0:T(8,128)(2,1)S(1)} %get-tuple-element.40), kind=kLoop, calls=%fused_computation | loop fusion | flops 6635520 | bytes 8847360 | tf_op jit(solution)/shard_map/concatenate | solution.py:291
  165.5 21.2 %shard_map.103 = bf16[1024,512]{1,0:T(8,128)(2,1)} custom-call(s32[16,1,1024]{2,1,0:T(1,128)S(1)} %fusion.25.slot_ref, f32[16,1,1024]{2,1,0:T(1,128)S(1)} %compare_select_fusion.14.weight_ref, bf16[16,72,1920]{2,1,0:T(8,128)(2,1)S(1)} %pad_maximum_fusion.sum_ref, bf16[16,512,640]{2,1,0:T(8,128)(2,1)S(1)} %bitcast.28, bf16[16,512,640]{2,1,0:T(8,128)(2,1)} %wu_ref.3), custom_call_target="tpu_custom_call" | custom-call | flops 2717908992 | bytes 20971520 | tf_op jit(solution)/shard_map/pallas_call | solution.py:203
  186.7 2.1 copy-done.1
  188.8 2.2 copy-done.2
  191.1 15.6 %shard_map.104 = (bf16[16,512,640]{2,1,0:T(8,128)(2,1)}, bf16[16,512,640]{2,1,0:T(8,128)(2,1)}, bf16[16,640,512]{2,1,0:T(8,128)(2,1)}) custom-call(s32[16,1,1024]{2,1,0:T(1,128)S(1)} %fusion.25.slot_ref, f32[16,1,1024]{2,1,0:T(1,128)S(1)} %compare_select_fusion.14.weight_ref, bf16[16,72,1024]{2,1,0:T(8,128)(2,1)S(1)} %get-tuple-element.10.rows_ref, ...), custom_call_target="tpu_custom_call" | custom-call | flops 2264924160 | bytes 31457280 | tf_op jit(solution)/shard_map/pallas_call | solution.py:231
  206.7 12.9 %reduce-scatter.2.cloned.1.call-done = bf16[128,512]{1,0:T(8,128)(2,1)} async-done(((bf16[1024,512]{1,0:T(8,128)(2,1)}), bf16[128,512]{1,0:T(8,128)(2,1)}) %reduce-scatter.2.cloned.1.call-update) | async-done | bytes 131088 | tf_op jit(solution)/shard_map/reduce_scatter | solution.py:328
  (80 shorter events, 19.7 us)
Async XLA Ops:
  7.2 39.6 %all-gather.2.cloned.1.call-start = ((), (), s32[]{:S(2)}) async-start(), calls=%async_computation.1 | async-start | bytes 2654208 | tf_op jit(solution)/shard_map/all_gather | solution.py:311
  12.3 207.3 %reduce-scatter.2.cloned.1.call-start = ((), (), s32[]{:S(2)}) async-start(), calls=%async_computation.2 | async-start | bytes 1179648 | tf_op jit(solution)/shard_map/reduce_scatter | solution.py:328
  12.4 42.6 %copy-start.18 = (f32[16]{0:T(128)}, f32[16]{0:T(128)S(1)}, u32[]{:S(2)}) copy-start(f32[16]{0:T(128)S(1)} %add_convert_fusion) | copy-start | bytes 196
  46.8 9.2 %copy-start.3 = (bf16[1024,1152]{1,0:T(8,128)(2,1)S(1)}, bf16[1024,1152]{1,0:T(8,128)(2,1)}, u32[]{:S(2)}) copy-start(bf16[1024,1152]{1,0:T(8,128)(2,1)} %all-gather.2.cloned.1.call-done.tok_ref) | copy-start | bytes 7077892
  47.9 8.0 %copy-start = (bf16[16,512,640]{2,1,0:T(8,128)(2,1)S(1)}, bf16[16,512,640]{2,1,0:T(8,128)(2,1)}, u32[]{:S(2)}) copy-start(bf16[16,512,640]{2,1,0:T(8,128)(2,1)} %wg_ref.3) | copy-start | bytes 31457284
  77.9 26.6 %collective-permute-start = (bf16[4,72,1920]{2,1,0:T(8,128)(2,1)S(1)}, bf16[4,72,1920]{2,1,0:T(8,128)(2,1)}, u32[]{:S(2)}, u32[]{:S(2)}) collective-permute-start(bf16[4,72,1920]{2,1,0:T(8,128)(2,1)S(1)} %dynamic-slice_bitcast_fusion.1), channel_id=1, source_target_pairs={{0,8},{8,0},{16,24},{24,16},{1,9},{9,1},{17,25},{25,17},{2,10},{10... | collective-permute-start | bytes 3317768 | tf_op jit(solution)/shard_map/ppermute | solution.py:256
  81.7 26.6 %collective-permute-start.4 = (bf16[4,72,1920]{2,1,0:T(8,128)(2,1)}, bf16[4,72,1920]{2,1,0:T(8,128)(2,1)}, u32[]{:S(2)}, u32[]{:S(2)}) collective-permute-start(bf16[4,72,1920]{2,1,0:T(8,128)(2,1)} %dynamic-slice_bitcast_fusion), channel_id=1, source_target_pairs={{0,16},{8,24},{16,0},{24,8},{1,17},{9,25},{17,1},{25,9},{2,18},{10... | collective-permute-start | bytes 3317768 | tf_op jit(solution)/shard_map/ppermute | solution.py:256
  104.5 3.7 %copy-start.4 = (bf16[8,72,1920]{2,1,0:T(8,128)(2,1)S(1)}, bf16[8,72,1920]{2,1,0:T(8,128)(2,1)}, u32[]{:S(2)}) copy-start(bf16[8,72,1920]{2,1,0:T(8,128)(2,1)} %get-tuple-element.39) | copy-start | bytes 6635524
  106.6 13.9 %collective-permute-start.1 = (bf16[2,72,1920]{2,1,0:T(8,128)(2,1)S(1)}, bf16[2,72,1920]{2,1,0:T(8,128)(2,1)S(1)}, u32[]{:S(2)}, u32[]{:S(2)}) collective-permute-start(bf16[2,72,1920]{2,1,0:T(8,128)(2,1)S(1)} %dynamic-slice_bitcast_fusion.3), channel_id=1, source_target_pairs={{0,16},{8,24},{16,0},{24,8},{1,17},{9,25},{17,1},{25,9},{2,18},{10... | collective-permute-start | bytes 1658888 | tf_op jit(solution)/shard_map/ppermute | solution.py:256
  110.6 13.9 %collective-permute-start.5 = (bf16[2,72,1920]{2,1,0:T(8,128)(2,1)}, bf16[2,72,1920]{2,1,0:T(8,128)(2,1)}, u32[]{:S(2)}, u32[]{:S(2)}) collective-permute-start(bf16[2,72,1920]{2,1,0:T(8,128)(2,1)} %dynamic-slice_bitcast_fusion.2), channel_id=1, source_target_pairs={{0,8},{8,0},{16,24},{24,16},{1,9},{9,1},{17,25},{25,17},{2,10},{10... | collective-permute-start | bytes 1658888 | tf_op jit(solution)/shard_map/ppermute | solution.py:256
  121.4 13.4 %collective-permute-start.2 = (bf16[2,72,1920]{2,1,0:T(8,128)(2,1)}, bf16[2,72,1920]{2,1,0:T(8,128)(2,1)}, u32[]{:S(2)}, u32[]{:S(2)}) collective-permute-start(bf16[2,72,1920]{2,1,0:T(8,128)(2,1)} %fusion.3), channel_id=1, source_target_pairs={{0,16},{8,24},{16,0},{24,8},{1,17},{9,25},{17,1},{25,9},{2,18},{10... | collective-permute-start | bytes 1658888 | tf_op jit(solution)/shard_map/ppermute | solution.py:256
  125.7 14.4 %collective-permute-start.6 = (bf16[2,72,1920]{2,1,0:T(8,128)(2,1)S(1)}, bf16[2,72,1920]{2,1,0:T(8,128)(2,1)S(1)}, u32[]{:S(2)}, u32[]{:S(2)}) collective-permute-start(bf16[2,72,1920]{2,1,0:T(8,128)(2,1)S(1)} %fusion.2), channel_id=1, source_target_pairs={{0,8},{8,0},{16,24},{24,16},{1,9},{9,1},{17,25},{25,17},{2,10},{10... | collective-permute-start | bytes 1658888 | tf_op jit(solution)/shard_map/ppermute | solution.py:256
  136.2 25.8 %collective-permute-start.3 = (bf16[4,72,1920]{2,1,0:T(8,128)(2,1)S(1)}, bf16[4,72,1920]{2,1,0:T(8,128)(2,1)S(1)}, u32[]{:S(2)}, u32[]{:S(2)}) collective-permute-start(bf16[4,72,1920]{2,1,0:T(8,128)(2,1)S(1)} %pad_maximum_fusion.1), channel_id=1, source_target_pairs={{0,8},{8,0},{16,24},{24,16},{1,9},{9,1},{17,25},{25,17},{2,10},{10... | collective-permute-start | bytes 3317768 | tf_op jit(solution)/shard_map/ppermute | solution.py:256
  140.1 2.0 copy-start.12
  140.1 2.0 copy-start.13
  140.1 2.0 copy-start.14
  140.1 2.0 copy-start.15
  140.1 2.0 copy-start.16
  140.2 25.2 %slice-start = ((s8[10485760]{0:T(1024)(128)(4,1)}), s8[4194304]{0:T(1024)(128)(4,1)S(1)}, s32[]{:S(2)}) async-start(s8[10485760]{0:T(1024)(128)(4,1)} %bitcast.27), calls=%async_computation.3 | async-start | bytes 8388608
  140.4 21.9 %collective-permute-start.7 = (bf16[4,72,1920]{2,1,0:T(8,128)(2,1)S(1)}, bf16[4,72,1920]{2,1,0:T(8,128)(2,1)S(1)}, u32[]{:S(2)}, u32[]{:S(2)}) collective-permute-start(bf16[4,72,1920]{2,1,0:T(8,128)(2,1)S(1)} %pad_maximum_fusion.2), channel_id=1, source_target_pairs={{0,16},{8,24},{16,0},{24,8},{1,17},{9,25},{17,1},{25,9},{2,18},{10... | collective-permute-start | bytes 3317768 | tf_op jit(solution)/shard_map/ppermute | solution.py:256
  142.5 23.0 %slice-start.1 = ((s8[10485760]{0:T(1024)(128)(4,1)}), s8[4194304]{0:T(1024)(128)(4,1)S(1)}, s32[]{:S(2)}) async-start(s8[10485760]{0:T(1024)(128)(4,1)} %bitcast.27), calls=%async_computation.4 | async-start | bytes 8388608
  162.6 2.9 %slice-start.2 = ((s8[10485760]{0:T(1024)(128)(4,1)}), s8[2097152]{0:T(1024)(128)(4,1)S(1)}, s32[]{:S(2)}) async-start(s8[10485760]{0:T(1024)(128)(4,1)} %bitcast.27), calls=%async_computation.5 | async-start | bytes 4194304
  186.7 2.1 copy-start.1
  188.8 2.3 copy-start.2
  (9 other events, 14.4 us)
Sparse Core Ops, SparseCore 0:
  12.4 34.3 all-gather.1
  189.0 30.5 reduce-scatter.1
